TPU v7x, 512 devices: a whole 4x4x16 slice. The times are simulated.
512 devices in a mesh: member: 8 (over x, core), space: 64 (over z, y).
Axes of the slice: x: 4, y: 4, z: 16, core: 2. Of those that a mesh axis runs over, the one named last changes fastest.
Arguments:
- initial_state: float32 [8, 256, 256, 256], P('member', 'space'), may hold values from -6 to 6
- final_cotangent: float32 [8, 256, 256, 256], P('member', 'space'), may hold values from -6 to 6
- legendre: bfloat16 [256, 256, 256], P('space'), may hold values from -0.375 to 0.375
- wave_map: int32 [256], replicated, may hold values from 0 to 255, each once
- column_list: int32 [64, 2048], P('space'), may hold values from 0 to 2047, each once within a row
- column_count: int32 [64], P('space'), may hold values from 1 to 512, 16384 in all
- weight_in: bfloat16 [128, 384], replicated, may hold values from -0.5 to 0.5
- bias_in: float32 [384], replicated, may hold values from -3 to 3
- weight_out: bfloat16 [384, 128], replicated, may hold values from -0.3125 to 0.3125
- bias_out: float32 [128], replicated, may hold values from -3 to 3
Outputs:
- grad_state: float32 [8, 256, 256, 256], P('member', 'space')
- grad_weight_in: float32 [128, 384], replicated
- grad_bias_in: float32 [384], replicated
- grad_weight_out: float32 [384, 128], replicated
- grad_bias_out: float32 [128], replicated
Inputs may be any that keep to these rules, and one draw needn't show every extreme that they name: Slot s of the spectral arrays and of legendre holds zonal wavenumber wave_map[s]; every wavenumber appears once. `column_list`: each row lists every local column of its band once; its first column_count entries are the band's active columns. `column_count`: the counts sum to 16384, and some band has exactly 512.
All inputs are finite; a program needn't handle non-finite values. No bound on the sum of `column_count` on one device may be relied on, other than what follows from the above.
Results may differ from a plain program's by a relative error of at most 0.0085.
Values may be sent and summed in bfloat16 or wider, within the bound.
No kernel may reach another device: no remote copies, remote signals or barrier semaphores. Data moves between devices by JAX's collectives and lax.ppermute only.
A program may use at most 64 MiB of HBM per device.

v0:
```python
import math

import jax
import jax.numpy as jnp
from jax import lax
from jax.sharding import PartitionSpec as P

LON = 512
ACT_DEV = 256
CAPA = 512


step_size = 0.5


def fourier_table(wave_ids, lon_count, total_waves):
    longitude = jnp.arange(lon_count, dtype=jnp.int32)
    phase_index = wave_ids[:, None] * longitude[None, :] % lon_count
    angles = phase_index.astype(jnp.float32) * (2.0 * math.pi / lon_count)
    norm_scale = 1.0 / math.sqrt(total_waves)
    stacked = jnp.stack([jnp.cos(angles), -jnp.sin(angles)], axis=1) * norm_scale
    return stacked.astype(jnp.bfloat16)


def spectral_factors(wave_ids, row_count, total_waves):
    degree = wave_ids[:, None] + jnp.arange(row_count, dtype=jnp.int32)[None, :]
    truncation = (degree < total_waves).astype(jnp.float32)
    degree_real = degree.astype(jnp.float32)
    damping = 1.0 / (1.0 + degree_real * (degree_real + 1.0) / (total_waves * (total_waves - 1.0)))
    return (damping[:, :, None], truncation[:, :, None])


def synthesis(legendre, coeffs):
    return jnp.einsum("sjl,sjc->slc", legendre, coeffs, preferred_element_type=jnp.float32)


def analysis(legendre, spectra):
    return jnp.einsum("sjl,slc->sjc", legendre, spectra, preferred_element_type=jnp.float32)


def fourier_synthesis(wave_table, spectra):
    shaped = spectra.reshape(spectra.shape[0], spectra.shape[1], 2, -1)
    return jnp.einsum("slpf,spn->lnf", shaped, wave_table, preferred_element_type=jnp.float32)


def fourier_analysis(wave_table, grid_band):
    result = jnp.einsum("lnf,spn->slpf", grid_band, wave_table, preferred_element_type=jnp.float32)
    return result.reshape(result.shape[0], result.shape[1], -1)


def silu_slope(preact):
    sigmoid_val = jax.nn.sigmoid(preact)
    return sigmoid_val * (1.0 + preact * (1.0 - sigmoid_val))


def send_band(spectra):
    return lax.all_to_all(spectra, "space", split_axis=1, concat_axis=0, tiled=True)


def tendency_home(spectra):
    return lax.all_to_all(spectra, "space", split_axis=0, concat_axis=1, tiled=True)


def adjoint_band(spectra):
    return lax.all_to_all(spectra, "space", split_axis=1, concat_axis=0, tiled=True)


def adjoint_home(spectra):
    return lax.all_to_all(spectra, "space", split_axis=0, concat_axis=1, tiled=True)


def body(
    initial_state,
    final_cotangent,
    legendre,
    wave_map,
    column_list,
    column_count,
    weight_in,
    bias_in,
    weight_out,
    bias_out,
):
    slot_count = legendre.shape[0]
    total_waves = wave_map.shape[0]
    wave_table = fourier_table(wave_map, LON, total_waves)
    own_waves = lax.dynamic_slice_in_dim(wave_map, lax.axis_index("space") * slot_count, slot_count)
    damping, truncation = spectral_factors(own_waves, legendre.shape[1], total_waves)
    index_list = column_list[0, :CAPA]
    valid_rows = (jnp.arange(CAPA, dtype=jnp.int32) < column_count[0]).astype(jnp.float32)[:, None]
    valid_half = valid_rows.astype(jnp.bfloat16)

    def physics_front(grid_band):
        columns = grid_band.reshape(-1, grid_band.shape[-1])
        inputs = jnp.take(columns, index_list, axis=0)
        preact = jnp.dot(inputs, weight_in, preferred_element_type=jnp.float32) + bias_in
        active = jax.nn.silu(preact).astype(jnp.bfloat16)
        return (inputs, preact, active)

    def physics_adjoint(adjoint_grid, stored):
        inputs, preact, active = stored
        columns = adjoint_grid.reshape(-1, adjoint_grid.shape[-1])
        adjoint_out = jnp.take(columns, index_list, axis=0) * valid_half
        grad_w_out = jnp.einsum(
            "ch,cf->hf", active, adjoint_out, preferred_element_type=jnp.float32
        )
        grad_b_out = jnp.sum(adjoint_out.astype(jnp.float32), axis=0)
        adjoint_act = jnp.einsum(
            "cf,hf->ch", adjoint_out, weight_out, preferred_element_type=jnp.float32
        )
        adjoint_pre = (adjoint_act * silu_slope(preact)).astype(jnp.bfloat16)
        grad_w_in = jnp.einsum("cf,ch->fh", inputs, adjoint_pre, preferred_element_type=jnp.float32)
        grad_b_in = jnp.sum(adjoint_pre.astype(jnp.float32), axis=0)
        adjoint_in = jnp.einsum(
            "ch,fh->cf", adjoint_pre, weight_in, preferred_element_type=jnp.float32
        ).astype(jnp.bfloat16)
        placed = jnp.zeros_like(columns).at[index_list].set(adjoint_in).reshape(adjoint_grid.shape)
        return (placed, (grad_w_in, grad_b_in, grad_w_out, grad_b_out))

    def adjoint_front(incoming):
        masked = truncation * incoming
        adjoint_source = (step_size * masked).astype(jnp.bfloat16)
        return (masked, synthesis(legendre, adjoint_source).astype(jnp.bfloat16))

    def adjoint_rest(masked, band_spectra, stored):
        adjoint_grid = fourier_synthesis(wave_table, band_spectra).astype(jnp.bfloat16)
        adjoint_cols, gradients = physics_adjoint(adjoint_grid, stored)
        back_spectra = fourier_analysis(wave_table, adjoint_cols).astype(jnp.bfloat16)
        return (damping * masked + analysis(legendre, adjoint_home(back_spectra)), gradients)

    coeffs_zero = initial_state[0]
    spectra_zero = synthesis(legendre, coeffs_zero.astype(jnp.bfloat16)).astype(jnp.bfloat16)
    grid_zero = fourier_synthesis(wave_table, send_band(spectra_zero)).astype(jnp.bfloat16)
    stored_zero = physics_front(grid_zero)
    grid_shape = grid_zero.shape
    output = (
        (jnp.dot(stored_zero[2], weight_out, preferred_element_type=jnp.float32) + bias_out)
        * valid_rows
    ).astype(jnp.bfloat16)
    placed = (
        jnp.zeros((grid_shape[0] * grid_shape[1], grid_shape[2]), jnp.bfloat16)
        .at[index_list]
        .set(output)
    )
    tendency_zero = placed.reshape(grid_shape)
    tendency_spectra = fourier_analysis(wave_table, tendency_zero).astype(jnp.bfloat16)
    coeffs_one = truncation * (
        damping * coeffs_zero + step_size * analysis(legendre, tendency_home(tendency_spectra))
    )
    spectra_one = synthesis(legendre, coeffs_one.astype(jnp.bfloat16)).astype(jnp.bfloat16)
    masked_two, adjoint_spectra_two = adjoint_front(final_cotangent[0])
    band_one = send_band(spectra_one)
    adjoint_band_two = adjoint_band(adjoint_spectra_two)
    grid_one = fourier_synthesis(wave_table, band_one).astype(jnp.bfloat16)
    stored_one = physics_front(grid_one)
    adjoint_one, grads_later = adjoint_rest(masked_two, adjoint_band_two, stored_one)
    masked_one, adjoint_spectra_one = adjoint_front(adjoint_one)
    adjoint_zero, grads_earlier = adjoint_rest(
        masked_one, adjoint_band(adjoint_spectra_one), stored_zero
    )
    local_totals = tuple((later + earlier for later, earlier in zip(grads_later, grads_earlier)))
    totals = lax.psum(
        (local_totals[0], local_totals[1], local_totals[2], local_totals[3]), ("member", "space")
    )
    norm_scale = 1.0 / math.sqrt(lax.axis_size("member") * lax.axis_size("space") * ACT_DEV)
    return (
        adjoint_zero[None],
        totals[0] * norm_scale,
        totals[1] * norm_scale,
        totals[2] * norm_scale,
        totals[3] * norm_scale,
    )


def solution(mesh):
    placed = (
        P("member", "space", None, None),
        P("member", "space", None, None),
        P("space", None, None),
        P(),
        P("space", None),
        P("space"),
        P(),
        P(),
        P(),
        P(),
    )
    return jax.shard_map(
        body,
        mesh=mesh,
        in_specs=placed,
        out_specs=(P("member", "space", None, None), P(), P(), P(), P()),
        check_vma=False,
    )
```

profile of v0, /device:TPU:6, one launch (start us, length us, event | category | flops | bytes accessed | tf_op | source)
XLA Modules:
  0.0 771.8 jit_solution(15844250548812017756)
XLA Ops:
  7.2 1.6 copy.100
  9.2 1.2 copy.103
  10.4 19.1 %all-to-all-start.1 = ((bf16[4,256,256]{2,0,1:T(4,128)(2,1)}), bf16[4,256,256]{2,0,1:T(4,128)(2,1)}, u32[]{:S(2)}, u32[]{:S(2)}) async-start(bf16[4,256,256]{2,0,1:T(4,128)(2,1)} %copy.103), calls=%async_computation.1 | async-start | bytes 1048576 | tf_op jit(solution)/shard_map/all_to_all | solution.py:57
  30.7 0.7 copy-done.25
  31.4 2.1 fusion.57
  33.6 28.6 %all-to-all-done.1 = bf16[4,256,256]{2,0,1:T(4,128)(2,1)} async-done(((bf16[4,256,256]{2,0,1:T(4,128)(2,1)}), bf16[4,256,256]{2,0,1:T(4,128)(2,1)}, u32[]{:S(2)}, u32[]{:S(2)}) %all-to-all-start.1) | async-done | bytes 524320 | tf_op jit(solution)/shard_map/all_to_all | solution.py:57
  62.2 1.2 copy.169
  64.1 1.3 gather_fusion.1
  65.5 1.2 multiply_convert_fusion.3
  67.7 1.9 scatter_custom_fusion
  70.2 1.1 copy.109
  71.2 6.1 all-to-all-start.2
  77.4 1.6 copy.96
  79.1 1.1 fusion.14
  80.2 2.1 copy.97
  82.3 27.0 %all-to-all-done.2 = bf16[256,4,256]{2,1,0:T(4,128)(2,1)} async-done(((bf16[256,4,256]{2,1,0:T(4,128)(2,1)}), bf16[256,4,256]{2,1,0:T(4,128)(2,1)}, u32[]{:S(2)}, u32[]{:S(2)}) %all-to-all-start.2) | async-done | bytes 524320 | tf_op jit(solution)/shard_map/all_to_all | solution.py:61
  109.2 6.3 all-to-all-start
  115.6 2.0 copy.110
  117.6 2.3 fusion.16
  120.0 2.1 copy.113
  122.1 25.1 %all-to-all-done = bf16[4,256,256]{2,0,1:T(4,128)(2,1)} async-done(((bf16[4,256,256]{2,0,1:T(4,128)(2,1)}), bf16[4,256,256]{2,0,1:T(4,128)(2,1)}, u32[]{:S(2)}, u32[]{:S(2)}) %all-to-all-start) | async-done | bytes 524320 | tf_op jit(solution)/shard_map/all_to_all | solution.py:65
  147.2 5.8 all-to-all-start.3
  153.1 1.2 copy.98
  154.3 1.0 reshape.237
  155.3 1.5 fusion.7
  156.8 1.9 gather_fusion
  158.7 26.4 %all-to-all-done.3 = bf16[4,256,256]{2,0,1:T(4,128)(2,1)S(1)} async-done(((bf16[4,256,256]{2,0,1:T(4,128)(2,1)}), bf16[4,256,256]{2,0,1:T(4,128)(2,1)S(1)}, u32[]{:S(2)}, u32[]{:S(2)}) %all-to-all-start.3) | async-done | bytes 524320 | tf_op jit(solution)/shard_map/all_to_all | solution.py:57
  185.3 1.0 reshape.242
  186.3 1.5 fusion.10
  187.8 1.3 gather_fusion.2
  190.5 1.1 convert_reduce_fusion.1
  191.8 2.1 scatter_custom_fusion.1
  194.7 37.7 %all_to_all.114 = bf16[256,4,256]{2,1,0:T(4,128)(2,1)S(1)} all-to-all(bf16[256,4,256]{2,1,0:T(4,128)(2,1)S(1)} %copy.119), channel_id=1, replica_groups=mesh['member'=8,'space'=64] {'space'}, dimensions={0} | all-to-all | bytes 1048576 | tf_op jit(solution)/shard_map/all_to_all | solution.py:69
  233.6 37.7 %all_to_all.115 = bf16[4,256,256]{2,0,1:T(4,128)(2,1)S(1)} all-to-all(bf16[4,256,256]{2,0,1:T(4,128)(2,1)S(1)} %copy.122), channel_id=1, replica_groups=mesh['member'=8,'space'=64] {'space'}, dimensions={1} | all-to-all | bytes 1048576 | tf_op jit(solution)/shard_map/all_to_all | solution.py:65
  272.2 1.3 gather_fusion.3
  274.1 2.3 convert_reduce_fusion
  276.7 2.1 scatter_custom_fusion.2
  279.3 1.1 copy.128
  280.3 6.0 all-to-all-start.6
  287.2 1.7 fusion.50
  289.8 0.7 copy-done.12
  290.5 1.0 convolution_add_fusion.4
  291.5 1.1 convolution_add_fusion.3
  292.7 104.4 %all-reduce = (f32[384]{0:T(512)S(1)}, f32[128]{0:T(128)S(1)}) all-reduce(f32[384]{0:T(512)S(1)} %add.159, f32[128]{0:T(128)S(1)} %add.161), channel_id=1, replica_groups=mesh['member'=8,'space'=64] {'member','space'}, use_global_device_ids=true, to_apply=%region_6.8 | all-reduce | flops 512 | bytes 4096 | tf_op jit(solution)/shard_map/psum | solution.py:162
  398.2 362.5 %all-reduce.4.cloned.1.call-done = (f32[128,384]{1,0:T(8,128)}, f32[384,128]{1,0:T(8,128)}) async-done(((f32[128,384]{1,0:T(8,128)}, f32[384,128]{1,0:T(8,128)}), (f32[128,384]{1,0:T(8,128)}, f32[384,128]{1,0:T(8,128)})) %all-reduce.4.cloned.1.call-update) | async-done | bytes 393232 | tf_op jit(solution)/shard_map/psum | solution.py:162
  760.7 1.7 broadcast_multiply_fusion.1
  762.4 0.7 broadcast_multiply_fusion
  763.7 1.3 copy.131
  (95 shorter events, 12.8 us)
Async XLA Ops:
  7.2 1.6 copy-start
  10.4 19.8 %copy-start.23 = (s32[1,2048]{1,0:T(1,128)S(1)}, s32[1,2048]{1,0:T(1,128)}, u32[]{:S(2)}) copy-start(s32[1,2048]{1,0:T(1,128)} %param.16) | copy-start | bytes 24580
  10.4 51.8 %all-to-all-start.1 = ((bf16[4,256,256]{2,0,1:T(4,128)(2,1)}), bf16[4,256,256]{2,0,1:T(4,128)(2,1)}, u32[]{:S(2)}, u32[]{:S(2)}) async-start(bf16[4,256,256]{2,0,1:T(4,128)(2,1)} %copy.103), calls=%async_computation.1 | async-start | bytes 1048576 | tf_op jit(solution)/shard_map/all_to_all | solution.py:57
  30.7 0.7 copy-start.25
  33.6 34.1 %copy-start.24 = (s32[512,1]{0,1:T(1,128)}, s32[512,1]{0,1:T(1,128)S(1)}, u32[]{:S(2)}) copy-start(s32[512,1]{0,1:T(1,128)S(1)} %compare_select_fusion) | copy-start | bytes 6148
  64.1 1.4 copy-start.7
  64.1 1.4 copy-start.20
  65.5 1.3 copy-start.11
  65.5 1.3 copy-start.16
  66.7 0.9 copy-start.1
  66.7 0.7 copy-start.26
  71.2 38.0 %all-to-all-start.2 = ((bf16[256,4,256]{2,1,0:T(4,128)(2,1)}), bf16[256,4,256]{2,1,0:T(4,128)(2,1)}, u32[]{:S(2)}, u32[]{:S(2)}) async-start(bf16[256,4,256]{2,1,0:T(4,128)(2,1)} %copy.109), calls=%async_computation.2 | async-start | bytes 1048576 | tf_op jit(solution)/shard_map/all_to_all | solution.py:61
  109.2 38.0 %all-to-all-start = ((bf16[4,256,256]{2,0,1:T(4,128)(2,1)}), bf16[4,256,256]{2,0,1:T(4,128)(2,1)}, u32[]{:S(2)}, u32[]{:S(2)}) async-start(bf16[4,256,256]{2,0,1:T(4,128)(2,1)} %copy.97), calls=%async_computation | async-start | bytes 1048576 | tf_op jit(solution)/shard_map/all_to_all | solution.py:65
  147.2 37.9 %all-to-all-start.3 = ((bf16[4,256,256]{2,0,1:T(4,128)(2,1)}), bf16[4,256,256]{2,0,1:T(4,128)(2,1)S(1)}, u32[]{:S(2)}, u32[]{:S(2)}) async-start(bf16[4,256,256]{2,0,1:T(4,128)(2,1)} %copy.113), calls=%async_computation.3 | async-start | bytes 1048576 | tf_op jit(solution)/shard_map/all_to_all | solution.py:57
  189.2 0.7 copy-start.3
  189.2 1.0 copy-start.13
  189.2 1.0 copy-start.17
  189.8 1.7 copy-start.10
  189.8 0.6 copy-start.18
  190.5 1.1 copy-start.8
  273.5 2.9 copy-start.5
  273.5 0.6 copy-start.19
  274.1 2.3 copy-start.9
  280.3 6.0 copy-start.4
  280.3 482.7 %all-to-all-start.6 = ((bf16[256,4,256]{2,1,0:T(4,128)(2,1)}), bf16[256,4,256]{2,1,0:T(4,128)(2,1)S(1)}, u32[]{:S(2)}, u32[]{:S(2)}) async-start(bf16[256,4,256]{2,1,0:T(4,128)(2,1)} %copy.128), calls=%async_computation.6 | async-start | bytes 1048576 | tf_op jit(solution)/shard_map/all_to_all | solution.py:69
  286.3 0.9 copy-start.14
  286.3 474.4 %all-reduce.4.cloned.1.call-start = ((), (), s32[]{:S(2)}) async-start(), calls=%async_computation.7 | async-start | bytes 786432 | tf_op jit(solution)/shard_map/psum | solution.py:162
  287.2 1.7 copy-start.22
  287.2 2.3 copy-start.6
  288.9 0.7 copy-start.21
  289.6 0.9 copy-start.12
  290.5 1.0 copy-start.2
  760.7 1.7 copy-start.15
Sparse Core Ops, SparseCore 0:
  293.1 467.5 all-reduce.3
where the time goes:
time: 773 us; the launch traced here: 772 us
  waiting for transfers between devices  470 us (61%)
  blocking collectives  180 us (23%)
  starting transfers between devices  43.3 us (6%)
  local copies, waits for them, and re-layouts  37.3 us (5%)
  matrix products  19.9 us (3%)
  between operations  15.2 us (2%)
    psum x1, waiting for transfers between devices, body(): lax.psum((local_totals[0], local_totals[1], local_totals[2], local_totals...  363 us
    psum x1, blocking collectives, body(): lax.psum((local_totals[0], local_totals[1], local_totals[2], local_totals...  104 us
    all_to_all x2, waiting for transfers between devices, send_band(): lax.all_to_all(spectra, 'space', split_axis=1, concat_axis=0, tiled=True)  55 us
    all_to_all x1, blocking collectives, adjoint_home(): lax.all_to_all(spectra, 'space', split_axis=0, concat_axis=1, tiled=True)  37.7 us
    all_to_all x1, blocking collectives, adjoint_band(): lax.all_to_all(spectra, 'space', split_axis=1, concat_axis=0, tiled=True)  37.7 us
    all_to_all x1, waiting for transfers between devices, tendency_home(): lax.all_to_all(spectra, 'space', split_axis=0, concat_axis=1, tiled=True)  27 us
    all_to_all x1, waiting for transfers between devices, adjoint_band(): lax.all_to_all(spectra, 'space', split_axis=1, concat_axis=0, tiled=True)  25.1 us
    all_to_all x2, starting transfers between devices, send_band(): lax.all_to_all(spectra, 'space', split_axis=1, concat_axis=0, tiled=True)  25 us
  transfers between devices with their start and end apart: 6, of which 5 were waited for; matrix products, arithmetic and copies ran while one was open for 4% of the time, Pallas kernels for 0%

commit v1 on v0

v1 whole, which is shorter than its diff:
```python
import math

import jax
import jax.numpy as jnp
from jax import lax
from jax.experimental import pallas as pl
from jax.experimental.pallas import tpu as pltpu
from jax.sharding import Mesh
from jax.sharding import PartitionSpec as P

LON = 512
CAPA = 512
WAVES = 256
F = 128
HID = 384
SPACE = 64
LATS = 4
SLOTS = 4
ROWS = LATS * SLOTS * 2
ACT_TOTAL = 131072
STEP = 0.5
SPACE_AXES = ("z", "y")
MEMBER_AXES = ("x", "core")
PLANE_AXES = ("x", "core", "y")
VMEM_LIMIT = 20 * 1024 * 1024

SMEM_SPEC = pl.BlockSpec(memory_space=pltpu.SMEM)
VMEM_SPEC = pl.BlockSpec(memory_space=pltpu.VMEM)


def kernel_params():
    return pltpu.CompilerParams(vmem_limit_bytes=VMEM_LIMIT)


def dot_last(a, b):
    return lax.dot_general(a, b, (((1,), (0,)), ((), ())), preferred_element_type=jnp.float32)


def dot_first(a, b):
    return lax.dot_general(a, b, (((0,), (0,)), ((), ())), preferred_element_type=jnp.float32)


def dot_rows(a, b):
    return lax.dot_general(a, b, (((1,), (1,)), ((), ())), preferred_element_type=jnp.float32)


def factors(wave):
    degree = wave + lax.broadcasted_iota(jnp.int32, (WAVES, F), 0)
    truncation = (degree < WAVES).astype(jnp.float32)
    degree_real = degree.astype(jnp.float32)
    damping = 1.0 / (1.0 + degree_real * (degree_real + 1.0) / (WAVES * (WAVES - 1.0)))
    both = lambda v: jnp.concatenate([v, v], axis=1)
    return both(damping), both(truncation)


def put_slot(rows, s, values):
    rows[pl.ds(2 * s, WAVES, stride=8), :] = values[:, :F]
    rows[pl.ds(2 * s + 1, WAVES, stride=8), :] = values[:, F:]


def get_slot(rows, s):
    parts = [rows[pl.ds(2 * s + p, WAVES, stride=8), :] for p in range(2)]
    return jnp.concatenate(parts, axis=1).astype(jnp.bfloat16)


def start_kernel(legendre, state, out, rows):
    for s in range(SLOTS):
        put_slot(rows, s, dot_first(legendre[s], state[s].astype(jnp.bfloat16)))
    out[...] = rows[...].astype(jnp.bfloat16).reshape(out.shape)


def cotangent_kernel(waves, legendre, state, out, rows):
    for s in range(SLOTS):
        _, truncation = factors(waves[s])
        source = (STEP * (truncation * state[s])).astype(jnp.bfloat16)
        put_slot(rows, s, dot_first(legendre[s], source))
    out[...] = rows[...].astype(jnp.bfloat16).reshape(out.shape)


def forward_home_kernel(waves, arrived, legendre, state, beside, out, taken, rows):
    taken[...] = arrived[...].reshape(taken.shape).astype(jnp.float32)
    for s in range(SLOTS):
        damping, truncation = factors(waves[s])
        tendency = dot_last(legendre[s], get_slot(taken, s))
        state_one = truncation * (damping * state[s] + STEP * tendency)
        put_slot(rows, s, dot_first(legendre[s], state_one.astype(jnp.bfloat16)))
    out[:, :ROWS, :] = rows[...].astype(jnp.bfloat16).reshape(SPACE, ROWS, F)
    out[:, ROWS:, :] = beside[...]


def adjoint_home_kernel(waves, arrived, legendre, cotangent, out, masked_out, taken, rows):
    taken[...] = arrived[...].reshape(taken.shape).astype(jnp.float32)
    for s in range(SLOTS):
        damping, truncation = factors(waves[s])
        outgoing = damping * (truncation * cotangent[s]) + dot_last(legendre[s], get_slot(taken, s))
        masked = truncation * outgoing
        masked_out[s] = masked
        put_slot(rows, s, dot_first(legendre[s], (STEP * masked).astype(jnp.bfloat16)))
    out[...] = rows[...].astype(jnp.bfloat16).reshape(out.shape)


def last_home_kernel(waves, arrived, legendre, masked, out, taken):
    taken[...] = arrived[...].reshape(taken.shape).astype(jnp.float32)
    for s in range(SLOTS):
        damping, _ = factors(waves[s])
        out[s] = damping * masked[s] + dot_last(legendre[s], get_slot(taken, s))


def forward_band_kernel(
    arrived, pick, place, weight_in, bias_in, weight_out, bias_out, out, inputs_out
):
    inputs = dot_last(pick[...], arrived[...].reshape(SPACE * ROWS, F)).astype(jnp.bfloat16)
    inputs_out[...] = inputs
    preact = dot_last(inputs, weight_in[...]) + bias_in[...]
    active = (preact * jax.nn.sigmoid(preact)).astype(jnp.bfloat16)
    tendency = (dot_last(active, weight_out[...]) + bias_out[...]).astype(jnp.bfloat16)
    out[...] = dot_last(place[...], tendency).astype(jnp.bfloat16).reshape(out.shape)


def physics_adjoint(inputs, adjoint_out, weight_in, bias_in, weight_out):
    preact = dot_last(inputs, weight_in) + bias_in
    sig = jax.nn.sigmoid(preact)
    active = (preact * sig).astype(jnp.bfloat16)
    slope = sig * (1.0 + preact * (1.0 - sig))
    adjoint_pre = (dot_rows(adjoint_out, weight_out) * slope).astype(jnp.bfloat16)
    adjoint_in = dot_rows(adjoint_pre, weight_in).astype(jnp.bfloat16)
    return active, adjoint_pre, adjoint_in


def gradients(inputs, active, adjoint_out, adjoint_pre):
    grad_in = dot_first(inputs, adjoint_pre)
    blocks = [grad_in[:, F * i : F * (i + 1)] for i in range(HID // F)]
    weights = jnp.concatenate(blocks + [dot_first(active, adjoint_out)], axis=0)
    bias_in = jnp.sum(adjoint_pre.astype(jnp.float32), axis=0, keepdims=True)
    bias_out = jnp.sum(adjoint_out.astype(jnp.float32), axis=0, keepdims=True)
    biases = [bias_in[:, F * i : F * (i + 1)] for i in range(HID // F)] + [bias_out]
    return weights, biases


def turn_band_kernel(arrived, pick, place, weight_in, bias_in, weight_out, out, grads_out):
    forward = arrived[:, :ROWS, :].reshape(SPACE * ROWS, F)
    adjoint = arrived[:, ROWS:, :].reshape(SPACE * ROWS, F)
    both = dot_last(pick[...], jnp.concatenate([forward, adjoint], axis=1)).astype(jnp.bfloat16)
    inputs, adjoint_out = both[:, :F], both[:, F:]
    active, adjoint_pre, adjoint_in = physics_adjoint(
        inputs, adjoint_out, weight_in[...], bias_in[...], weight_out[...]
    )
    out[...] = dot_last(place[...], adjoint_in).astype(jnp.bfloat16).reshape(out.shape)
    weights, biases = gradients(inputs, active, adjoint_out, adjoint_pre)
    grads_out[...] = jnp.zeros_like(grads_out)
    grads_out[:, :24, :] = weights.reshape(32, 24, F)
    for i, row in enumerate(biases):
        grads_out[i, 24:25, :] = row


def last_band_kernel(
    arrived, pick, place, inputs_ref, weight_in, bias_in, weight_out, earlier, out, grads_out, total
):
    adjoint = arrived[...].reshape(SPACE * ROWS, F)
    adjoint_out = dot_last(pick[...], adjoint).astype(jnp.bfloat16)
    inputs = inputs_ref[...]
    active, adjoint_pre, adjoint_in = physics_adjoint(
        inputs, adjoint_out, weight_in[...], bias_in[...], weight_out[...]
    )
    out[...] = dot_last(place[...], adjoint_in).astype(jnp.bfloat16).reshape(out.shape)
    weights, biases = gradients(inputs, active, adjoint_out, adjoint_pre)
    total[...] = earlier[...]
    total[:, :24, :] = earlier[:, :24, :] + weights.reshape(32, 24, F)
    for i, row in enumerate(biases):
        total[i, 24:25, :] = earlier[i, 24:25, :] + row
    grads_out[...] = total[...].astype(jnp.bfloat16)


def plane_sum_kernel(parts, out):
    total = jnp.sum(parts[...].astype(jnp.float32), axis=0, keepdims=True)
    out[...] = jnp.broadcast_to(total.astype(jnp.bfloat16), out.shape)


def unpack_kernel(whole, grad_in, grad_bias_in, grad_out, grad_bias_out):
    weights = whole[:, :24, :].reshape(768, F)
    for i in range(3):
        grad_in[:, F * i : F * (i + 1)] = weights[F * i : F * (i + 1)]
        grad_bias_in[:, F * i : F * (i + 1)] = whole[i, 24:25, :]
    grad_out[...] = weights[HID:]
    grad_bias_out[...] = whole[3, 24:25, :]


def call(kernel, outs, specs, scratch=(), name=None):
    return pl.pallas_call(
        kernel,
        out_shape=outs,
        in_specs=specs,
        out_specs=jax.tree.map(lambda _: VMEM_SPEC, outs),
        scratch_shapes=list(scratch),
        compiler_params=kernel_params(),
        name=name,
    )


def travel(block):
    return lax.all_to_all(block, SPACE_AXES, split_axis=0, concat_axis=0, tiled=True)


def fourier_table(wave_ids):
    longitude = jnp.arange(LON, dtype=jnp.int32)
    phase_index = wave_ids[:, None] * longitude[None, :] % LON
    angles = phase_index.astype(jnp.float32) * (2.0 * math.pi / LON)
    norm_scale = 1.0 / math.sqrt(WAVES)
    stacked = jnp.stack([jnp.cos(angles), -jnp.sin(angles)], axis=1) * norm_scale
    return stacked.astype(jnp.bfloat16)


def column_matrices(wave_map, column_list, column_count):
    table = fourier_table(wave_map).reshape(SPACE, 1, SLOTS * 2, LON)
    table = jnp.broadcast_to(table, (SPACE, LATS, SLOTS * 2, LON)).reshape(SPACE * ROWS, LON)
    columns = column_list[0, :CAPA]
    valid = jnp.arange(CAPA, dtype=jnp.int32) < column_count[0]
    longitude = jnp.arange(LON, dtype=jnp.int32)
    chosen = (columns % LON)[:, None] == longitude[None, :]
    chosen = (chosen & valid[:, None]).astype(jnp.bfloat16)
    row_lat = (jnp.arange(SPACE * ROWS, dtype=jnp.int32) // (SLOTS * 2)) % LATS
    slot_lat = columns // LON
    pick = jnp.einsum("cn,rn->cr", chosen, table, preferred_element_type=jnp.float32)
    pick = jnp.where(slot_lat[:, None] == row_lat[None, :], pick, 0.0).astype(jnp.bfloat16)
    place = jnp.einsum("rn,cn->rc", table, chosen, preferred_element_type=jnp.float32)
    place = jnp.where(row_lat[:, None] == slot_lat[None, :], place, 0.0).astype(jnp.bfloat16)
    return pick, place


def body(
    initial_state,
    final_cotangent,
    legendre,
    wave_map,
    column_list,
    column_count,
    weight_in,
    bias_in,
    weight_out,
    bias_out,
):
    own = lax.axis_index(SPACE_AXES) * SLOTS
    waves = lax.dynamic_slice_in_dim(wave_map, own, SLOTS)
    state, cotangent = initial_state[0], final_cotangent[0]
    bias_in, bias_out = bias_in[None], bias_out[None]
    block = jax.ShapeDtypeStruct((SPACE, ROWS, F), jnp.bfloat16)
    wide = jax.ShapeDtypeStruct((SPACE, 2 * ROWS, F), jnp.bfloat16)
    full = jax.ShapeDtypeStruct((SLOTS, WAVES, 2 * F), jnp.float32)
    grads = jax.ShapeDtypeStruct((32, 32, F), jnp.float32)
    rows = pltpu.VMEM((SPACE * ROWS, F), jnp.float32)
    V, S = VMEM_SPEC, SMEM_SPEC

    spectra_zero = call(start_kernel, block, [V, V], [rows], "state_synthesis")(legendre, state)
    band_zero = travel(spectra_zero)
    pick, place = column_matrices(wave_map, column_list, column_count)
    adjoint_two = call(cotangent_kernel, block, [S, V, V], [rows], "cotangent_synthesis")(
        waves, legendre, cotangent
    )
    tendency, inputs_zero = call(
        forward_band_kernel,
        (block, jax.ShapeDtypeStruct((CAPA, F), jnp.bfloat16)),
        [V] * 7,
        name="physics_forward",
    )(band_zero, pick, place, weight_in, bias_in, weight_out, bias_out)
    both = call(forward_home_kernel, wide, [S, V, V, V, V], [rows, rows], "state_step")(
        waves, travel(tendency), legendre, state, adjoint_two
    )
    back_two, grads_two = call(turn_band_kernel, (block, grads), [V] * 6, name="physics_turn")(
        travel(both), pick, place, weight_in, bias_in, weight_out
    )
    adjoint_one, masked_one = call(
        adjoint_home_kernel, (block, full), [S, V, V, V], [rows, rows], "adjoint_step"
    )(waves, travel(back_two), legendre, cotangent)
    back_one, grads_all = call(
        last_band_kernel,
        (block, jax.ShapeDtypeStruct((32, 32, F), jnp.bfloat16)),
        [V] * 8,
        [pltpu.VMEM((32, 32, F), jnp.float32)],
        "physics_adjoint",
    )(travel(adjoint_one), pick, place, inputs_zero, weight_in, bias_in, weight_out, grads_two)

    parts = lax.all_to_all(grads_all, PLANE_AXES, split_axis=0, concat_axis=0, tiled=True)
    copies = call(
        plane_sum_kernel, jax.ShapeDtypeStruct((16, 32, F), jnp.bfloat16), [V], name="plane_sum"
    )(parts)
    pieces = lax.all_to_all(copies, "z", split_axis=0, concat_axis=0, tiled=True)
    piece = jnp.sum(pieces.astype(jnp.float32), axis=0) * (1.0 / math.sqrt(ACT_TOTAL))
    whole = lax.all_gather(lax.all_gather(piece[None], "y", tiled=True), MEMBER_AXES, tiled=True)
    shape = lambda *dims: jax.ShapeDtypeStruct(dims, jnp.float32)
    grad_weight_in, grad_bias_in, grad_weight_out, grad_bias_out = call(
        unpack_kernel, (shape(F, HID), shape(1, HID), shape(HID, F), shape(1, F)), [V], name="unpack"
    )(whole)

    grad_state = call(last_home_kernel, full, [S, V, V, V], [rows], "last_analysis")(
        waves, travel(back_one), legendre, masked_one
    )

    return (
        grad_state[None],
        grad_weight_in,
        grad_bias_in[0],
        grad_weight_out,
        grad_bias_out[0],
    )


def solution(mesh):
    fine = Mesh(mesh.devices.reshape(4, 2, 16, 4), ("x", "core", "z", "y"))
    member, space = ("x", "core"), ("z", "y")
    return jax.shard_map(
        body,
        mesh=fine,
        in_specs=(
            P(member, space, None, None),
            P(member, space, None, None),
            P(space, None, None),
            P(),
            P(space, None),
            P(space),
            P(),
            P(),
            P(),
            P(),
        ),
        out_specs=(P(member, space, None, None), P(), P(), P(), P()),
        check_vma=False,
    )
```

time: 773 us -> 318 us (0.41)
  waiting for transfers between devices: 470 us -> 59 us
  local copies, waits for them, and re-layouts: 37.3 us -> 8.11 us
  Pallas kernels: 0 us -> 17.3 us
  matrix products: 19.9 us -> 4.5 us
  between operations: 15.2 us -> 1.54 us
  starting transfers between devices: 43.3 us -> 31.2 us
  blocking collectives: 180 us -> 191 us
    psum x1 -> x0, waiting for transfers between devices: 363 us -> none  [body(): lax.psum((local_totals[0], local_totals[1], local_totals[2], local_totals...]
    psum x1 -> x0, blocking collectives: 104 us -> none  [body(): lax.psum((local_totals[0], local_totals[1], local_totals[2], local_totals...]
    all_to_all x2 -> x5, blocking collectives: 75.4 us -> 165 us  [the longest x3 134 us: travel(): lax.all_to_all(block, SPACE_AXES, split_axis=0, concat_axis=0, tiled=True)]
    all_to_all x5 -> x3, waiting for transfers between devices: 107 us -> 59 us  [travel(): lax.all_to_all(block, SPACE_AXES, split_axis=0, concat_axis=0, tiled=True)]
    all_gather x0 -> x2, blocking collectives: none -> 25.5 us  [the longest x1 13.1 us: body(): lax.all_gather(lax.all_gather(piece[None], 'y', tiled=True), MEMBER_AXES,...]
    pallas_call x0 -> x10, Pallas kernels: none -> 17.3 us  [the longest x1 3.53 us: body(): call(last_band_kernel, (block, jax.ShapeDtypeStruct((32, 32, F), jnp.bflo...]
    dot_general x24 -> x2, matrix products: 19.9 us -> 4.5 us  [the longest x1 2.79 us: column_matrices(): jnp.einsum('rn,cn->rc', table, chosen, preferred_element_type=jnp.float32)]
    all_to_all x5 -> x3, starting transfers between devices: 43.3 us -> 31.2 us  [travel(): lax.all_to_all(block, SPACE_AXES, split_axis=0, concat_axis=0, tiled=True)]
  transfers between devices with their start and end apart: 6 -> 3, of which waited for: 5 -> 3; matrix products, arithmetic and copies ran while one was open for 4% -> 3% of each run, Pallas kernels for 0% -> 1%
where the time goes in v1:
time: 318 us; the launch traced here: 316 us
  blocking collectives  191 us (60%)
  waiting for transfers between devices  59 us (19%)
  starting transfers between devices  31.2 us (10%)
  Pallas kernels  17.3 us (5%)
  local copies, waits for them, and re-layouts  8.11 us (3%)
  matrix products  4.5 us (1%)
  other arithmetic  3.61 us (1%)
    all_to_all x3, blocking collectives, travel(): lax.all_to_all(block, SPACE_AXES, split_axis=0, concat_axis=0, tiled=True)  134 us
    all_to_all x3, waiting for transfers between devices, travel(): lax.all_to_all(block, SPACE_AXES, split_axis=0, concat_axis=0, tiled=True)  59 us
    all_to_all x3, starting transfers between devices, travel(): lax.all_to_all(block, SPACE_AXES, split_axis=0, concat_axis=0, tiled=True)  31.2 us
    all_to_all x1, blocking collectives, body(): lax.all_to_all(copies, 'z', split_axis=0, concat_axis=0, tiled=True)  16.7 us
    all_to_all x1, blocking collectives, body(): lax.all_to_all(grads_all, PLANE_AXES, split_axis=0, concat_axis=0, tiled=...  14.3 us
    all_gather x1, blocking collectives, body(): lax.all_gather(lax.all_gather(piece[None], 'y', tiled=True), MEMBER_AXES,...  13.1 us
    all_gather x1, blocking collectives, body(): lax.all_gather(piece[None], 'y', tiled=True)  12.5 us
    unnamed x32, local copies, waits for them, and re-layouts  7.14 us
  transfers between devices with their start and end apart: 3, of which 3 were waited for; matrix products, arithmetic and copies ran while one was open for 3% of the time, Pallas kernels for 1%

profile of v1, /device:TPU:6, one launch (start us, length us, event | category | flops | bytes accessed | tf_op | source)
XLA Modules:
  0.0 315.9 jit_solution(17363837407945416543)
XLA Ops:
  0.6 0.0 copy-start.2
  0.7 1.0 copy-done.2
  1.7 1.2 copy-done.6
  2.9 1.2 state_synthesis.1
  4.1 18.7 %all-to-all-start = ((bf16[64,32,128]{2,1,0:T(8,128)(2,1)}), bf16[64,32,128]{2,1,0:T(8,128)(2,1)S(1)}, u32[]{:S(2)}, u32[]{:S(2)}) async-start(bf16[64,32,128]{2,1,0:T(8,128)(2,1)} %state_synthesis.1), calls=%async_computation | async-start | bytes 1048576 | tf_op jit(solution)/shard_map/all_to_all | solution.py:201
  22.9 0.0 copy-done.15
  22.9 2.1 fusion.14
  25.0 0.0 copy-start.14
  25.0 0.1 fusion
  25.2 0.5 copy.15
  25.7 0.2 convert_element_type.36
  26.6 0.7 and_select_fusion
  27.3 0.2 broadcast_in_dim.15
  27.5 1.7 select_convert_fusion.1.pick
  29.2 0.0 copy-start.10
  29.2 0.0 copy-start.11
  29.2 0.0 copy-start.13
  29.3 2.8 select_convert_fusion.place
  32.0 23.6 %all-to-all-done.arrived = bf16[64,32,128]{2,1,0:T(8,128)(2,1)S(1)} async-done(((bf16[64,32,128]{2,1,0:T(8,128)(2,1)}), bf16[64,32,128]{2,1,0:T(8,128)(2,1)S(1)}, u32[]{:S(2)}, u32[]{:S(2)}) %all-to-all-start) | async-done | bytes 524320 | tf_op jit(solution)/shard_map/all_to_all | solution.py:201
  55.7 0.0 copy-start
  55.7 1.6 copy-done
  57.3 2.6 physics_forward.1
  59.9 0.0 copy-start.12
  59.9 0.8 copy-done.12
  60.7 6.1 %all-to-all-start.1 = ((bf16[64,32,128]{2,1,0:T(8,128)(2,1)}), bf16[64,32,128]{2,1,0:T(8,128)(2,1)}, u32[]{:S(2)}, u32[]{:S(2)}) async-start(bf16[64,32,128]{2,1,0:T(8,128)(2,1)} %copy-done.12), calls=%async_computation.1 | async-start | bytes 1048576 | tf_op jit(solution)/shard_map/all_to_all | solution.py:201
  66.8 0.1 dynamic_slice.3.waves
  66.9 0.0 copy-done.3
  66.9 1.2 copy-done.4
  68.1 1.0 cotangent_synthesis.1.beside
  69.1 29.6 %all-to-all-done.1.arrived = bf16[64,32,128]{2,1,0:T(8,128)(2,1)} async-done(((bf16[64,32,128]{2,1,0:T(8,128)(2,1)}), bf16[64,32,128]{2,1,0:T(8,128)(2,1)}, u32[]{:S(2)}, u32[]{:S(2)}) %all-to-all-start.1) | async-done | bytes 524320 | tf_op jit(solution)/shard_map/all_to_all | solution.py:201
  98.7 1.2 copy-done.7
  99.9 2.0 state_step.1
  101.9 60.2 %all_to_all.40.arrived = bf16[64,64,128]{2,1,0:T(8,128)(2,1)S(1)} all-to-all(bf16[64,64,128]{2,1,0:T(8,128)(2,1)S(1)} %state_step.1), channel_id=1, replica_groups=mesh['x'=4,'core'=2,'z'=16,'y'=4] {'z','y'}, dimensions={0} | all-to-all | bytes 2097152 | tf_op jit(solution)/shard_map/all_to_all | solution.py:201
  162.1 2.9 physics_turn.1
  165.0 37.1 %all_to_all.41.arrived = bf16[64,32,128]{2,1,0:T(8,128)(2,1)S(1)} all-to-all(bf16[64,32,128]{2,1,0:T(8,128)(2,1)S(1)} %get-tuple-element.18), channel_id=1, replica_groups=mesh['x'=4,'core'=2,'z'=16,'y'=4] {'z','y'}, dimensions={0} | all-to-all | bytes 1048576 | tf_op jit(solution)/shard_map/all_to_all | solution.py:201
  202.1 1.3 adjoint_step.1
  203.4 0.0 copy-start.8
  203.4 36.9 %all_to_all.42.arrived = bf16[64,32,128]{2,1,0:T(8,128)(2,1)S(1)} all-to-all(bf16[64,32,128]{2,1,0:T(8,128)(2,1)S(1)} %get-tuple-element.19), channel_id=1, replica_groups=mesh['x'=4,'core'=2,'z'=16,'y'=4] {'z','y'}, dimensions={0} | all-to-all | bytes 1048576 | tf_op jit(solution)/shard_map/all_to_all | solution.py:201
  240.4 3.5 %physics_adjoint.1 = (bf16[64,32,128]{2,1,0:T(8,128)(2,1)}, bf16[32,32,128]{2,1,0:T(8,128)(2,1)S(1)}) custom-call(bf16[64,32,128]{2,1,0:T(8,128)(2,1)S(1)} %all_to_all.42.arrived, bf16[512,2048]{1,0:T(8,128)(2,1)S(1)} %select_convert_fusion.1.pick, bf16[2048,512]{1,0:T(8,128)(2,1)S(1)} %copy-done.1, bf16[512,128]{1,0:T(8,128)(2,1)S(1)} %get-tuple-element.20.inputs_ref, ...), custom_call_target="tpu_custom_call" | custom-call | tf_op jit(solution)/shard_map/physics_adjoint/pallas_call | solution.py:274
  243.9 14.3 %all_to_all.43.parts = bf16[32,32,128]{2,1,0:T(8,128)(2,1)S(1)} all-to-all(bf16[32,32,128]{2,1,0:T(8,128)(2,1)S(1)} %get-tuple-element.24), channel_id=1, replica_groups=mesh['x'=4,'core'=2,'z'=16,'y'=4] {'x','core','y'}, dimensions={0} | all-to-all | bytes 524288 | tf_op jit(solution)/shard_map/all_to_all | solution.py:282
  258.2 16.7 %all_to_all.44 = bf16[16,32,128]{2,1,0:T(8,128)(2,1)S(1)} all-to-all(bf16[16,32,128]{2,1,0:T(8,128)(2,1)S(1)} %plane_sum.1), channel_id=1, replica_groups=mesh['x'=4,'core'=2,'z'=16,'y'=4] {'z'}, dimensions={0} | all-to-all | bytes 262144 | tf_op jit(solution)/shard_map/all_to_all | solution.py:286
  274.9 6.3 %all-to-all-start.5 = ((bf16[64,32,128]{2,1,0:T(8,128)(2,1)}), bf16[64,32,128]{2,1,0:T(8,128)(2,1)S(1)}, u32[]{:S(2)}, u32[]{:S(2)}) async-start(bf16[64,32,128]{2,1,0:T(8,128)(2,1)} %get-tuple-element.22), calls=%async_computation.5 | async-start | bytes 1048576 | tf_op jit(solution)/shard_map/all_to_all | solution.py:201
  281.3 12.5 %all-gather = f32[128,128]{1,0:T(8,128)S(1)} all-gather(f32[32,128]{1,0:T(8,128)S(1)} %broadcast_multiply_fusion), channel_id=2, replica_groups=mesh['x'=4,'core'=2,'z'=16,'y'=4] {'y'}, dimensions={0}, use_global_device_ids=true | all-gather | bytes 81920 | tf_op jit(solution)/shard_map/all_gather | solution.py:288
  293.8 13.1 %all_gather.7.whole = f32[32,32,128]{2,1,0:T(8,128)S(1)} all-gather(f32[4,32,128]{2,1,0:T(8,128)S(1)} %bitcast.21), channel_id=1, replica_groups=mesh['x'=4,'core'=2,'z'=16,'y'=4] {'x','core'}, dimensions={0}, use_global_device_ids=true | all-gather | bytes 589824 | tf_op jit(solution)/shard_map/all_gather | solution.py:288
  306.8 0.8 unpack.1
  307.6 0.6 reduce
  308.2 5.7 %all-to-all-done.5.arrived = bf16[64,32,128]{2,1,0:T(8,128)(2,1)S(1)} async-done(((bf16[64,32,128]{2,1,0:T(8,128)(2,1)}), bf16[64,32,128]{2,1,0:T(8,128)(2,1)S(1)}, u32[]{:S(2)}, u32[]{:S(2)}) %all-to-all-start.5) | async-done | bytes 524320 | tf_op jit(solution)/shard_map/all_to_all | solution.py:201
  314.0 2.0 last_analysis.1
  (23 shorter events, 0.1 us)
Async XLA Ops:
  0.6 22.2 %copy-start.15 = (s32[256]{0:T(256)S(1)}, s32[256]{0:T(256)}, u32[]{:S(2)}) copy-start(s32[256]{0:T(256)} %param.13) | copy-start | bytes 3076
  0.6 1.0 copy-start.2
  1.7 1.2 copy-start.6
  4.1 51.6 %all-to-all-start = ((bf16[64,32,128]{2,1,0:T(8,128)(2,1)}), bf16[64,32,128]{2,1,0:T(8,128)(2,1)S(1)}, u32[]{:S(2)}, u32[]{:S(2)}) async-start(bf16[64,32,128]{2,1,0:T(8,128)(2,1)} %state_synthesis.1), calls=%async_computation | async-start | bytes 1048576 | tf_op jit(solution)/shard_map/all_to_all | solution.py:201
  25.0 1.5 copy-start.14
  29.2 26.5 %copy-start.10 = (bf16[128,384]{1,0:T(8,128)(2,1)S(1)}, bf16[128,384]{1,0:T(8,128)(2,1)}, u32[]{:S(2)}) copy-start(bf16[128,384]{1,0:T(8,128)(2,1)} %weight_in.5) | copy-start | bytes 294916
  29.2 26.5 %copy-start.11 = (bf16[384,128]{1,0:T(8,128)(2,1)S(1)}, bf16[384,128]{1,0:T(8,128)(2,1)}, u32[]{:S(2)}) copy-start(bf16[384,128]{1,0:T(8,128)(2,1)} %weight_out.5) | copy-start | bytes 294916
  29.2 26.5 %copy-start.13 = (f32[128]{0:T(128)S(1)}, f32[128]{0:T(128)}, u32[]{:S(2)}) copy-start(f32[128]{0:T(128)} %param.19) | copy-start | bytes 1540
  55.7 1.6 copy-start
  57.3 9.6 %copy-start.3 = (bf16[4,256,256]{2,1,0:T(8,128)(2,1)S(1)}, bf16[4,256,256]{2,1,0:T(8,128)(2,1)}, u32[]{:S(2)}) copy-start(bf16[4,256,256]{2,1,0:T(8,128)(2,1)} %legendre.9) | copy-start | bytes 1572868
  59.9 0.8 copy-start.12
  60.7 38.0 %all-to-all-start.1 = ((bf16[64,32,128]{2,1,0:T(8,128)(2,1)}), bf16[64,32,128]{2,1,0:T(8,128)(2,1)}, u32[]{:S(2)}, u32[]{:S(2)}) async-start(bf16[64,32,128]{2,1,0:T(8,128)(2,1)} %copy-done.12), calls=%async_computation.1 | async-start | bytes 1048576 | tf_op jit(solution)/shard_map/all_to_all | solution.py:201
  66.9 1.2 copy-start.4
  98.7 1.2 copy-start.7
  99.9 62.1 %copy-start.1 = (bf16[2048,512]{1,0:T(8,128)(2,1)S(1)}, bf16[2048,512]{1,0:T(8,128)(2,1)}, u32[]{:S(2)}) copy-start(bf16[2048,512]{1,0:T(8,128)(2,1)} %select_convert_fusion.place) | copy-start | bytes 6291460
  162.1 40.0 %copy-start.5 = (f32[1,4,256,256]{3,2,1,0:T(8,128)S(1)}, f32[1,4,256,256]{3,2,1,0:T(8,128)}, u32[]{:S(2)}) copy-start(f32[1,4,256,256]{3,2,1,0:T(8,128)} %param.11) | copy-start | bytes 3145732
  203.4 40.5 %copy-start.8 = (f32[4,256,256]{2,1,0:T(8,128)}, f32[4,256,256]{2,1,0:T(8,128)S(1)}, u32[]{:S(2)}) copy-start(f32[4,256,256]{2,1,0:T(8,128)S(1)} %get-tuple-element.23.masked) | copy-start | bytes 3145732
  243.9 70.1 %copy-start.9 = (f32[4,256,256]{2,1,0:T(8,128)S(1)}, f32[4,256,256]{2,1,0:T(8,128)}, u32[]{:S(2)}) copy-start(f32[4,256,256]{2,1,0:T(8,128)} %copy-done.8) | copy-start | bytes 3145732
  274.9 39.0 %all-to-all-start.5 = ((bf16[64,32,128]{2,1,0:T(8,128)(2,1)}), bf16[64,32,128]{2,1,0:T(8,128)(2,1)S(1)}, u32[]{:S(2)}, u32[]{:S(2)}) async-start(bf16[64,32,128]{2,1,0:T(8,128)(2,1)} %get-tuple-element.22), calls=%async_computation.5 | async-start | bytes 1048576 | tf_op jit(solution)/shard_map/all_to_all | solution.py:201

commit v2 on v1

--- a/solution.py
+++ b/solution.py
@@ -22,7 +22,7 @@
 SPACE_AXES = ("z", "y")
 MEMBER_AXES = ("x", "core")
 PLANE_AXES = ("x", "core", "y")
-VMEM_LIMIT = 20 * 1024 * 1024
+VMEM_LIMIT = 16 * 1024 * 1024
 
 SMEM_SPEC = pl.BlockSpec(memory_space=pltpu.SMEM)
 VMEM_SPEC = pl.BlockSpec(memory_space=pltpu.VMEM)
@@ -63,8 +63,22 @@
     return jnp.concatenate(parts, axis=1).astype(jnp.bfloat16)
 
 
-def start_kernel(legendre, state, out, rows):
-    for s in range(SLOTS):
+def fetch(sources, targets, sems):
+    copies = [
+        [pltpu.make_async_copy(src.at[s], dst.at[s], sems.at[i, s]) for s in range(SLOTS)]
+        for i, (src, dst) in enumerate(zip(sources, targets))
+    ]
+    for s in range(SLOTS):
+        for one in copies:
+            one[s].start()
+    return copies
+
+
+def start_kernel(legendre_hbm, state_hbm, out, rows, legendre, state, sems):
+    copies = fetch((legendre_hbm, state_hbm), (legendre, state), sems)
+    for s in range(SLOTS):
+        for one in copies:
+            one[s].wait()
         put_slot(rows, s, dot_first(legendre[s], state[s].astype(jnp.bfloat16)))
     out[...] = rows[...].astype(jnp.bfloat16).reshape(out.shape)
 
@@ -99,11 +113,16 @@
     out[...] = rows[...].astype(jnp.bfloat16).reshape(out.shape)
 
 
-def last_home_kernel(waves, arrived, legendre, masked, out, taken):
+def last_home_kernel(waves, arrived, legendre, masked, out_hbm, taken, out, sems):
     taken[...] = arrived[...].reshape(taken.shape).astype(jnp.float32)
+    copies = []
     for s in range(SLOTS):
         damping, _ = factors(waves[s])
         out[s] = damping * masked[s] + dot_last(legendre[s], get_slot(taken, s))
+        copies.append(pltpu.make_async_copy(out.at[s], out_hbm.at[s], sems.at[s]))
+        copies[s].start()
+    for copy in copies:
+        copy.wait()
 
 
 def forward_band_kernel(
@@ -154,7 +173,7 @@
 
 
 def last_band_kernel(
-    arrived, pick, place, inputs_ref, weight_in, bias_in, weight_out, earlier, out, grads_out, total
+    arrived, pick, inputs_ref, weight_in, bias_in, weight_out, earlier, adj_in_out, grads_out, total
 ):
     adjoint = arrived[...].reshape(SPACE * ROWS, F)
     adjoint_out = dot_last(pick[...], adjoint).astype(jnp.bfloat16)
@@ -162,13 +181,17 @@
     active, adjoint_pre, adjoint_in = physics_adjoint(
         inputs, adjoint_out, weight_in[...], bias_in[...], weight_out[...]
     )
-    out[...] = dot_last(place[...], adjoint_in).astype(jnp.bfloat16).reshape(out.shape)
+    adj_in_out[...] = adjoint_in
     weights, biases = gradients(inputs, active, adjoint_out, adjoint_pre)
     total[...] = earlier[...]
     total[:, :24, :] = earlier[:, :24, :] + weights.reshape(32, 24, F)
     for i, row in enumerate(biases):
         total[i, 24:25, :] = earlier[i, 24:25, :] + row
     grads_out[...] = total[...].astype(jnp.bfloat16)
+
+
+def place_kernel(place, values, out):
+    out[...] = dot_last(place[...], values[...]).astype(jnp.bfloat16).reshape(out.shape)
 
 
 def plane_sum_kernel(parts, out):
@@ -185,16 +208,24 @@
     grad_bias_out[...] = whole[3, 24:25, :]
 
 
-def call(kernel, outs, specs, scratch=(), name=None):
+def call(kernel, outs, specs, scratch=(), name=None, out_specs=None):
     return pl.pallas_call(
         kernel,
         out_shape=outs,
         in_specs=specs,
-        out_specs=jax.tree.map(lambda _: VMEM_SPEC, outs),
+        out_specs=out_specs or jax.tree.map(lambda _: VMEM_SPEC, outs),
         scratch_shapes=list(scratch),
         compiler_params=kernel_params(),
         name=name,
     )
+
+
+def in_hbm(x):
+    return pltpu.with_memory_space_constraint(x, pltpu.HBM)
+
+
+def in_vmem(x):
+    return pltpu.with_memory_space_constraint(x, pltpu.VMEM)
 
 
 def travel(block):
@@ -243,24 +274,32 @@
     waves = lax.dynamic_slice_in_dim(wave_map, own, SLOTS)
     state, cotangent = initial_state[0], final_cotangent[0]
     bias_in, bias_out = bias_in[None], bias_out[None]
-    block = jax.ShapeDtypeStruct((SPACE, ROWS, F), jnp.bfloat16)
-    wide = jax.ShapeDtypeStruct((SPACE, 2 * ROWS, F), jnp.bfloat16)
+    block = pltpu.VMEM((SPACE, ROWS, F), jnp.bfloat16)
+    narrow = pltpu.VMEM((CAPA, F), jnp.bfloat16)
+    wide = pltpu.VMEM((SPACE, 2 * ROWS, F), jnp.bfloat16)
     full = jax.ShapeDtypeStruct((SLOTS, WAVES, 2 * F), jnp.float32)
-    grads = jax.ShapeDtypeStruct((32, 32, F), jnp.float32)
+    kept = pltpu.VMEM((SLOTS, WAVES, 2 * F), jnp.float32)
+    grads = pltpu.VMEM((32, 32, F), jnp.float32)
     rows = pltpu.VMEM((SPACE * ROWS, F), jnp.float32)
-    V, S = VMEM_SPEC, SMEM_SPEC
-
-    spectra_zero = call(start_kernel, block, [V, V], [rows], "state_synthesis")(legendre, state)
+    copied = pltpu.VMEM((SLOTS, WAVES, 2 * F), jnp.float32)
+    sems = lambda *shape: pltpu.SemaphoreType.DMA(shape)
+    V, S, A = VMEM_SPEC, SMEM_SPEC, pl.BlockSpec(memory_space=pltpu.HBM)
+
+    spectra_zero = call(
+        start_kernel,
+        block,
+        [A, A],
+        [rows, pltpu.VMEM((SLOTS, WAVES, WAVES), jnp.bfloat16), copied, sems(2, SLOTS)],
+        "state_synthesis",
+    )(in_hbm(legendre), in_hbm(state))
     band_zero = travel(spectra_zero)
-    pick, place = column_matrices(wave_map, column_list, column_count)
+    pick, place = map(in_vmem, column_matrices(wave_map, column_list, column_count))
     adjoint_two = call(cotangent_kernel, block, [S, V, V], [rows], "cotangent_synthesis")(
         waves, legendre, cotangent
     )
+    band_zero, adjoint_two = lax.optimization_barrier((band_zero, adjoint_two))
     tendency, inputs_zero = call(
-        forward_band_kernel,
-        (block, jax.ShapeDtypeStruct((CAPA, F), jnp.bfloat16)),
-        [V] * 7,
-        name="physics_forward",
+        forward_band_kernel, (block, narrow), [V] * 7, name="physics_forward"
     )(band_zero, pick, place, weight_in, bias_in, weight_out, bias_out)
     both = call(forward_home_kernel, wide, [S, V, V, V, V], [rows, rows], "state_step")(
         waves, travel(tendency), legendre, state, adjoint_two
@@ -269,17 +308,22 @@
         travel(both), pick, place, weight_in, bias_in, weight_out
     )
     adjoint_one, masked_one = call(
-        adjoint_home_kernel, (block, full), [S, V, V, V], [rows, rows], "adjoint_step"
+        adjoint_home_kernel, (block, kept), [S, V, V, V], [rows, rows], "adjoint_step"
     )(waves, travel(back_two), legendre, cotangent)
-    back_one, grads_all = call(
+    adjoint_in, grads_all = call(
         last_band_kernel,
-        (block, jax.ShapeDtypeStruct((32, 32, F), jnp.bfloat16)),
-        [V] * 8,
+        (
+            narrow,
+            pltpu.VMEM((32, 32, F), jnp.bfloat16),
+        ),
+        [V] * 7,
         [pltpu.VMEM((32, 32, F), jnp.float32)],
         "physics_adjoint",
-    )(travel(adjoint_one), pick, place, inputs_zero, weight_in, bias_in, weight_out, grads_two)
+    )(travel(adjoint_one), pick, inputs_zero, weight_in, bias_in, weight_out, grads_two)
 
     parts = lax.all_to_all(grads_all, PLANE_AXES, split_axis=0, concat_axis=0, tiled=True)
+    back_one = call(place_kernel, block, [V, V], name="place_adjoint")(place, adjoint_in)
+    arrived = travel(back_one)
     copies = call(
         plane_sum_kernel, jax.ShapeDtypeStruct((16, 32, F), jnp.bfloat16), [V], name="plane_sum"
     )(parts)
@@ -291,9 +335,9 @@
         unpack_kernel, (shape(F, HID), shape(1, HID), shape(HID, F), shape(1, F)), [V], name="unpack"
     )(whole)
 
-    grad_state = call(last_home_kernel, full, [S, V, V, V], [rows], "last_analysis")(
-        waves, travel(back_one), legendre, masked_one
-    )
+    grad_state = call(
+        last_home_kernel, full, [S, V, V, V], [rows, copied, sems(SLOTS)], "last_analysis", A
+    )(waves, arrived, legendre, masked_one)
 
     return (
         grad_state[None],

time: 318 us -> 315 us (level)
  blocking collectives: 191 us -> 212 us
  waiting for transfers between devices: 59 us -> 40.3 us
  local copies, waits for them, and re-layouts: 8.11 us -> 4.35 us
    all_to_all x3 -> x4, blocking collectives: 134 us -> 172 us  [travel(): lax.all_to_all(block, SPACE_AXES, split_axis=0, concat_axis=0, tiled=True)]
    all_to_all x3 -> x2, waiting for transfers between devices: 59 us -> 27.9 us  [travel(): lax.all_to_all(block, SPACE_AXES, split_axis=0, concat_axis=0, tiled=True)]
    all_to_all x1 -> x0, blocking collectives: 16.7 us -> none  [body(): lax.all_to_all(copies, 'z', split_axis=0, concat_axis=0, tiled=True)]
    all_to_all x0 -> x1, waiting for transfers between devices: none -> 12.5 us  [body(): lax.all_to_all(copies, 'z', split_axis=0, concat_axis=0, tiled=True)]
    all_to_all x3 -> x2, starting transfers between devices: 31.2 us -> 25.2 us  [travel(): lax.all_to_all(block, SPACE_AXES, split_axis=0, concat_axis=0, tiled=True)]
    unnamed x32 -> x30, local copies, waits for them, and re-layouts: 7.14 us -> 3.38 us
    all_to_all x0 -> x1, starting transfers between devices: none -> 3.51 us  [body(): lax.all_to_all(copies, 'z', split_axis=0, concat_axis=0, tiled=True)]
    pallas_call x5 -> x6, Pallas kernels: 10.6 us -> 12.2 us  [the longest x1 2.89 us: body(): call(start_kernel, block, [A, A], [rows, pltpu.VMEM((SLOTS, WAVES, WAVES)...]
where the time goes in v2:
time: 315 us; the launch traced here: 313 us
  blocking collectives  212 us (67%)
  waiting for transfers between devices  40.3 us (13%)
  starting transfers between devices  28.7 us (9%)
  Pallas kernels  18.9 us (6%)
  local copies, waits for them, and re-layouts  4.35 us (1%)
  matrix products  4.12 us (1%)
  other arithmetic  3.61 us (1%)
    all_to_all x4, blocking collectives, travel(): lax.all_to_all(block, SPACE_AXES, split_axis=0, concat_axis=0, tiled=True)  172 us
    all_to_all x2, waiting for transfers between devices, travel(): lax.all_to_all(block, SPACE_AXES, split_axis=0, concat_axis=0, tiled=True)  27.9 us
    all_to_all x2, starting transfers between devices, travel(): lax.all_to_all(block, SPACE_AXES, split_axis=0, concat_axis=0, tiled=True)  25.2 us
    all_to_all x1, blocking collectives, body(): lax.all_to_all(grads_all, PLANE_AXES, split_axis=0, concat_axis=0, tiled=...  14.2 us
    all_gather x1, blocking collectives, body(): lax.all_gather(lax.all_gather(piece[None], 'y', tiled=True), MEMBER_AXES,...  13.1 us
    all_to_all x1, waiting for transfers between devices, body(): lax.all_to_all(copies, 'z', split_axis=0, concat_axis=0, tiled=True)  12.5 us
    all_gather x1, blocking collectives, body(): lax.all_gather(piece[None], 'y', tiled=True)  12.5 us
  transfers between devices with their start and end apart: 3, of which 3 were waited for; matrix products, arithmetic and copies ran while one was open for 3% of the time, Pallas kernels for 1%

profile of v2, /device:TPU:6, one launch (start us, length us, event | category | flops | bytes accessed | tf_op | source)
XLA Modules:
  0.0 313.2 jit_solution(14135115980448516131)
XLA Ops:
  0.6 0.0 copy-start.14
  0.6 2.9 state_synthesis.1
  3.5 18.7 %all-to-all-start = ((bf16[64,32,128]{2,1,0:T(8,128)(2,1)}), bf16[64,32,128]{2,1,0:T(8,128)(2,1)S(1)}, u32[]{:S(2)}, u32[]{:S(2)}) async-start(bf16[64,32,128]{2,1,0:T(8,128)(2,1)} %state_synthesis.1), calls=%async_computation | async-start | bytes 1048576 | tf_op jit(solution)/shard_map/all_to_all | solution.py:232
  22.3 0.0 copy-done.14
  22.3 0.1 dynamic_slice.3.waves
  22.4 2.1 fusion.14
  24.5 0.0 copy-start.13
  24.5 0.0 copy-start.2
  24.6 0.0 copy-start.3
  24.6 0.1 fusion
  24.7 0.5 copy.15
  25.2 0.2 convert_element_type.36
  26.1 0.0 copy-done.13
  26.1 0.0 copy-done.2
  26.1 0.0 copy-done.3
  26.1 1.0 cotangent_synthesis.1.beside
  27.1 0.0 copy-start.6
  27.1 0.8 copy-done.6
  27.9 0.7 fusion.20
  28.6 0.2 broadcast_in_dim.15
  28.8 2.7 select_convert_fusion.pick
  31.5 1.4 select_convert_fusion.1.place
  32.9 22.2 %all-to-all-done.arrived = bf16[64,32,128]{2,1,0:T(8,128)(2,1)S(1)} async-done(((bf16[64,32,128]{2,1,0:T(8,128)(2,1)}), bf16[64,32,128]{2,1,0:T(8,128)(2,1)S(1)}, u32[]{:S(2)}, u32[]{:S(2)}) %all-to-all-start) | async-done | bytes 524320 | tf_op jit(solution)/shard_map/all_to_all | solution.py:232
  55.1 0.0 copy-start
  55.1 1.6 copy-done
  56.7 2.6 physics_forward.1
  59.3 37.7 %all_to_all.40.arrived = bf16[64,32,128]{2,1,0:T(8,128)(2,1)S(1)} all-to-all(bf16[64,32,128]{2,1,0:T(8,128)(2,1)S(1)} %get-tuple-element.20), channel_id=1, replica_groups=mesh['x'=4,'core'=2,'z'=16,'y'=4] {'z','y'}, dimensions={0} | all-to-all | bytes 1048576 | tf_op jit(solution)/shard_map/all_to_all | solution.py:232
  97.0 1.3 state_step.1
  98.4 60.2 %all_to_all.41.arrived = bf16[64,64,128]{2,1,0:T(8,128)(2,1)S(1)} all-to-all(bf16[64,64,128]{2,1,0:T(8,128)(2,1)S(1)} %state_step.1), channel_id=1, replica_groups=mesh['x'=4,'core'=2,'z'=16,'y'=4] {'z','y'}, dimensions={0} | all-to-all | bytes 2097152 | tf_op jit(solution)/shard_map/all_to_all | solution.py:232
  158.5 2.9 physics_turn.1
  161.5 37.1 %all_to_all.42.arrived = bf16[64,32,128]{2,1,0:T(8,128)(2,1)S(1)} all-to-all(bf16[64,32,128]{2,1,0:T(8,128)(2,1)S(1)} %get-tuple-element.22), channel_id=1, replica_groups=mesh['x'=4,'core'=2,'z'=16,'y'=4] {'z','y'}, dimensions={0} | all-to-all | bytes 1048576 | tf_op jit(solution)/shard_map/all_to_all | solution.py:232
  198.5 1.4 adjoint_step.1
  199.9 0.0 copy-start.8
  199.9 1.0 copy-done.8
  200.9 36.9 %all_to_all.43.arrived = bf16[64,32,128]{2,1,0:T(8,128)(2,1)S(1)} all-to-all(bf16[64,32,128]{2,1,0:T(8,128)(2,1)S(1)} %get-tuple-element.23), channel_id=1, replica_groups=mesh['x'=4,'core'=2,'z'=16,'y'=4] {'z','y'}, dimensions={0} | all-to-all | bytes 1048576 | tf_op jit(solution)/shard_map/all_to_all | solution.py:232
  237.8 1.9 physics_adjoint.1
  239.7 14.2 %all_to_all.44.parts = bf16[32,32,128]{2,1,0:T(8,128)(2,1)S(1)} all-to-all(bf16[32,32,128]{2,1,0:T(8,128)(2,1)S(1)} %get-tuple-element.28), channel_id=1, replica_groups=mesh['x'=4,'core'=2,'z'=16,'y'=4] {'x','core','y'}, dimensions={0} | all-to-all | bytes 524288 | tf_op jit(solution)/shard_map/all_to_all | solution.py:324
  253.9 0.7 plane_sum.1
  254.6 3.5 %all-to-all-start.7 = ((bf16[16,32,128]{2,1,0:T(8,128)(2,1)}), bf16[16,32,128]{2,1,0:T(8,128)(2,1)S(1)}, u32[]{:S(2)}, u32[]{:S(2)}) async-start(bf16[16,32,128]{2,1,0:T(8,128)(2,1)} %plane_sum.1), calls=%async_computation.7 | async-start | bytes 262144 | tf_op jit(solution)/shard_map/all_to_all | solution.py:330
  258.1 1.5 place_adjoint.1
  259.6 12.5 %all-to-all-done.7 = bf16[16,32,128]{2,1,0:T(8,128)(2,1)S(1)} async-done(((bf16[16,32,128]{2,1,0:T(8,128)(2,1)}), bf16[16,32,128]{2,1,0:T(8,128)(2,1)S(1)}, u32[]{:S(2)}, u32[]{:S(2)}) %all-to-all-start.7) | async-done | bytes 131104 | tf_op jit(solution)/shard_map/all_to_all | solution.py:330
  272.0 6.4 %all-to-all-start.5 = ((bf16[64,32,128]{2,1,0:T(8,128)(2,1)}), bf16[64,32,128]{2,1,0:T(8,128)(2,1)S(1)}, u32[]{:S(2)}, u32[]{:S(2)}) async-start(bf16[64,32,128]{2,1,0:T(8,128)(2,1)} %place_adjoint.1), calls=%async_computation.5 | async-start | bytes 1048576 | tf_op jit(solution)/shard_map/all_to_all | solution.py:232
  278.5 12.5 %all-gather = f32[128,128]{1,0:T(8,128)S(1)} all-gather(f32[32,128]{1,0:T(8,128)S(1)} %broadcast_multiply_fusion), channel_id=2, replica_groups=mesh['x'=4,'core'=2,'z'=16,'y'=4] {'y'}, dimensions={0}, use_global_device_ids=true | all-gather | bytes 81920 | tf_op jit(solution)/shard_map/all_gather | solution.py:332
  291.0 13.1 %all_gather.7.whole = f32[32,32,128]{2,1,0:T(8,128)S(1)} all-gather(f32[4,32,128]{2,1,0:T(8,128)S(1)} %bitcast.21), channel_id=1, replica_groups=mesh['x'=4,'core'=2,'z'=16,'y'=4] {'x','core'}, dimensions={0}, use_global_device_ids=true | all-gather | bytes 589824 | tf_op jit(solution)/shard_map/all_gather | solution.py:332
  304.1 0.8 unpack.1
  304.8 0.6 reduce
  305.4 5.7 %all-to-all-done.5.arrived = bf16[64,32,128]{2,1,0:T(8,128)(2,1)S(1)} async-done(((bf16[64,32,128]{2,1,0:T(8,128)(2,1)}), bf16[64,32,128]{2,1,0:T(8,128)(2,1)S(1)}, u32[]{:S(2)}, u32[]{:S(2)}) %all-to-all-start.5) | async-done | bytes 524320 | tf_op jit(solution)/shard_map/all_to_all | solution.py:232
  311.2 1.9 last_analysis.1
  (22 shorter events, 0.1 us)
Async XLA Ops:
  0.6 21.7 %copy-start.14 = (s32[256]{0:T(256)S(1)}, s32[256]{0:T(256)}, u32[]{:S(2)}) copy-start(s32[256]{0:T(256)} %param.13) | copy-start | bytes 3076
  3.5 51.6 %all-to-all-start = ((bf16[64,32,128]{2,1,0:T(8,128)(2,1)}), bf16[64,32,128]{2,1,0:T(8,128)(2,1)S(1)}, u32[]{:S(2)}, u32[]{:S(2)}) async-start(bf16[64,32,128]{2,1,0:T(8,128)(2,1)} %state_synthesis.1), calls=%async_computation | async-start | bytes 1048576 | tf_op jit(solution)/shard_map/all_to_all | solution.py:232
  24.5 1.6 copy-start.13
  24.5 1.6 copy-start.2
  24.6 1.6 copy-start.3
  27.1 0.8 copy-start.6
  31.5 23.6 %copy-start.10 = (bf16[128,384]{1,0:T(8,128)(2,1)S(1)}, bf16[128,384]{1,0:T(8,128)(2,1)}, u32[]{:S(2)}) copy-start(bf16[128,384]{1,0:T(8,128)(2,1)} %weight_in.5) | copy-start | bytes 294916
  31.5 23.6 %copy-start.11 = (bf16[384,128]{1,0:T(8,128)(2,1)S(1)}, bf16[384,128]{1,0:T(8,128)(2,1)}, u32[]{:S(2)}) copy-start(bf16[384,128]{1,0:T(8,128)(2,1)} %weight_out.5) | copy-start | bytes 294916
  31.5 23.6 %copy-start.12 = (f32[128]{0:T(128)S(1)}, f32[128]{0:T(128)}, u32[]{:S(2)}) copy-start(f32[128]{0:T(128)} %param.19) | copy-start | bytes 1540
  55.1 1.6 copy-start
  56.7 40.3 %copy-start.5 = (f32[1,4,256,256]{3,2,1,0:T(8,128)S(1)}, f32[1,4,256,256]{3,2,1,0:T(8,128)}, u32[]{:S(2)}) copy-start(f32[1,4,256,256]{3,2,1,0:T(8,128)} %param.10) | copy-start | bytes 3145732
  56.7 40.3 %copy-start.7 = (bf16[64,32,128]{2,1,0:T(8,128)(2,1)S(1)}, bf16[64,32,128]{2,1,0:T(8,128)(2,1)}, u32[]{:S(2)}) copy-start(bf16[64,32,128]{2,1,0:T(8,128)(2,1)} %copy-done.6) | copy-start | bytes 1572868
  97.0 61.5 %copy-start.1 = (bf16[512,2048]{1,0:T(8,128)(2,1)S(1)}, bf16[512,2048]{1,0:T(8,128)(2,1)}, u32[]{:S(2)}) copy-start(bf16[512,2048]{1,0:T(8,128)(2,1)} %select_convert_fusion.pick) | copy-start | bytes 6291460
  158.5 40.0 %copy-start.4 = (f32[1,4,256,256]{3,2,1,0:T(8,128)S(1)}, f32[1,4,256,256]{3,2,1,0:T(8,128)}, u32[]{:S(2)}) copy-start(f32[1,4,256,256]{3,2,1,0:T(8,128)} %param.11) | copy-start | bytes 3145732
  199.9 1.0 copy-start.8
  254.6 17.5 %all-to-all-start.7 = ((bf16[16,32,128]{2,1,0:T(8,128)(2,1)}), bf16[16,32,128]{2,1,0:T(8,128)(2,1)S(1)}, u32[]{:S(2)}, u32[]{:S(2)}) async-start(bf16[16,32,128]{2,1,0:T(8,128)(2,1)} %plane_sum.1), calls=%async_computation.7 | async-start | bytes 262144 | tf_op jit(solution)/shard_map/all_to_all | solution.py:330
  259.6 51.6 %copy-start.9 = (f32[4,256,256]{2,1,0:T(8,128)S(1)}, f32[4,256,256]{2,1,0:T(8,128)}, u32[]{:S(2)}) copy-start(f32[4,256,256]{2,1,0:T(8,128)} %copy-done.8) | copy-start | bytes 3145732
  272.0 39.1 %all-to-all-start.5 = ((bf16[64,32,128]{2,1,0:T(8,128)(2,1)}), bf16[64,32,128]{2,1,0:T(8,128)(2,1)S(1)}, u32[]{:S(2)}, u32[]{:S(2)}) async-start(bf16[64,32,128]{2,1,0:T(8,128)(2,1)} %place_adjoint.1), calls=%async_computation.5 | async-start | bytes 1048576 | tf_op jit(solution)/shard_map/all_to_all | solution.py:232

commit v3 on v2

--- a/solution.py
+++ b/solution.py
@@ -22,7 +22,7 @@
 SPACE_AXES = ("z", "y")
 MEMBER_AXES = ("x", "core")
 PLANE_AXES = ("x", "core", "y")
-VMEM_LIMIT = 16 * 1024 * 1024
+VMEM_LIMIT = 12 * 1024 * 1024
 
 SMEM_SPEC = pl.BlockSpec(memory_space=pltpu.SMEM)
 VMEM_SPEC = pl.BlockSpec(memory_space=pltpu.VMEM)
@@ -42,6 +42,10 @@
 
 def dot_rows(a, b):
     return lax.dot_general(a, b, (((1,), (1,)), ((), ())), preferred_element_type=jnp.float32)
+
+
+def placed(pick, values, shape):
+    return dot_first(values, pick).T.astype(jnp.bfloat16).reshape(shape)
 
 
 def factors(wave):
@@ -126,14 +130,14 @@
 
 
 def forward_band_kernel(
-    arrived, pick, place, weight_in, bias_in, weight_out, bias_out, out, inputs_out
+    arrived, pick, weight_in, bias_in, weight_out, bias_out, out, inputs_out
 ):
     inputs = dot_last(pick[...], arrived[...].reshape(SPACE * ROWS, F)).astype(jnp.bfloat16)
     inputs_out[...] = inputs
     preact = dot_last(inputs, weight_in[...]) + bias_in[...]
     active = (preact * jax.nn.sigmoid(preact)).astype(jnp.bfloat16)
     tendency = (dot_last(active, weight_out[...]) + bias_out[...]).astype(jnp.bfloat16)
-    out[...] = dot_last(place[...], tendency).astype(jnp.bfloat16).reshape(out.shape)
+    out[...] = placed(pick[...], tendency, out.shape)
 
 
 def physics_adjoint(inputs, adjoint_out, weight_in, bias_in, weight_out):
@@ -156,7 +160,7 @@
     return weights, biases
 
 
-def turn_band_kernel(arrived, pick, place, weight_in, bias_in, weight_out, out, grads_out):
+def turn_band_kernel(arrived, pick, weight_in, bias_in, weight_out, out, grads_out):
     forward = arrived[:, :ROWS, :].reshape(SPACE * ROWS, F)
     adjoint = arrived[:, ROWS:, :].reshape(SPACE * ROWS, F)
     both = dot_last(pick[...], jnp.concatenate([forward, adjoint], axis=1)).astype(jnp.bfloat16)
@@ -164,7 +168,7 @@
     active, adjoint_pre, adjoint_in = physics_adjoint(
         inputs, adjoint_out, weight_in[...], bias_in[...], weight_out[...]
     )
-    out[...] = dot_last(place[...], adjoint_in).astype(jnp.bfloat16).reshape(out.shape)
+    out[...] = placed(pick[...], adjoint_in, out.shape)
     weights, biases = gradients(inputs, active, adjoint_out, adjoint_pre)
     grads_out[...] = jnp.zeros_like(grads_out)
     grads_out[:, :24, :] = weights.reshape(32, 24, F)
@@ -190,8 +194,8 @@
     grads_out[...] = total[...].astype(jnp.bfloat16)
 
 
-def place_kernel(place, values, out):
-    out[...] = dot_last(place[...], values[...]).astype(jnp.bfloat16).reshape(out.shape)
+def place_kernel(pick, values, out):
+    out[...] = placed(pick[...], values[...], out.shape)
 
 
 def plane_sum_kernel(parts, out):
@@ -203,9 +207,9 @@
     weights = whole[:, :24, :].reshape(768, F)
     for i in range(3):
         grad_in[:, F * i : F * (i + 1)] = weights[F * i : F * (i + 1)]
-        grad_bias_in[:, F * i : F * (i + 1)] = whole[i, 24:25, :]
+        grad_bias_in[F * i : F * (i + 1)] = whole[i, 24, :]
     grad_out[...] = weights[HID:]
-    grad_bias_out[...] = whole[3, 24:25, :]
+    grad_bias_out[...] = whole[3, 24, :]
 
 
 def call(kernel, outs, specs, scratch=(), name=None, out_specs=None):
@@ -241,7 +245,7 @@
     return stacked.astype(jnp.bfloat16)
 
 
-def column_matrices(wave_map, column_list, column_count):
+def column_matrix(wave_map, column_list, column_count):
     table = fourier_table(wave_map).reshape(SPACE, 1, SLOTS * 2, LON)
     table = jnp.broadcast_to(table, (SPACE, LATS, SLOTS * 2, LON)).reshape(SPACE * ROWS, LON)
     columns = column_list[0, :CAPA]
@@ -253,9 +257,7 @@
     slot_lat = columns // LON
     pick = jnp.einsum("cn,rn->cr", chosen, table, preferred_element_type=jnp.float32)
     pick = jnp.where(slot_lat[:, None] == row_lat[None, :], pick, 0.0).astype(jnp.bfloat16)
-    place = jnp.einsum("rn,cn->rc", table, chosen, preferred_element_type=jnp.float32)
-    place = jnp.where(row_lat[:, None] == slot_lat[None, :], place, 0.0).astype(jnp.bfloat16)
-    return pick, place
+    return pick
 
 
 def body(
@@ -293,19 +295,19 @@
         "state_synthesis",
     )(in_hbm(legendre), in_hbm(state))
     band_zero = travel(spectra_zero)
-    pick, place = map(in_vmem, column_matrices(wave_map, column_list, column_count))
+    pick = in_vmem(column_matrix(wave_map, column_list, column_count))
     adjoint_two = call(cotangent_kernel, block, [S, V, V], [rows], "cotangent_synthesis")(
         waves, legendre, cotangent
     )
     band_zero, adjoint_two = lax.optimization_barrier((band_zero, adjoint_two))
     tendency, inputs_zero = call(
-        forward_band_kernel, (block, narrow), [V] * 7, name="physics_forward"
-    )(band_zero, pick, place, weight_in, bias_in, weight_out, bias_out)
+        forward_band_kernel, (block, narrow), [V] * 6, name="physics_forward"
+    )(band_zero, pick, weight_in, bias_in, weight_out, bias_out)
     both = call(forward_home_kernel, wide, [S, V, V, V, V], [rows, rows], "state_step")(
         waves, travel(tendency), legendre, state, adjoint_two
     )
-    back_two, grads_two = call(turn_band_kernel, (block, grads), [V] * 6, name="physics_turn")(
-        travel(both), pick, place, weight_in, bias_in, weight_out
+    back_two, grads_two = call(turn_band_kernel, (block, grads), [V] * 5, name="physics_turn")(
+        travel(both), pick, weight_in, bias_in, weight_out
     )
     adjoint_one, masked_one = call(
         adjoint_home_kernel, (block, kept), [S, V, V, V], [rows, rows], "adjoint_step"
@@ -322,7 +324,7 @@
     )(travel(adjoint_one), pick, inputs_zero, weight_in, bias_in, weight_out, grads_two)
 
     parts = lax.all_to_all(grads_all, PLANE_AXES, split_axis=0, concat_axis=0, tiled=True)
-    back_one = call(place_kernel, block, [V, V], name="place_adjoint")(place, adjoint_in)
+    back_one = call(place_kernel, block, [V, V], name="place_adjoint")(pick, adjoint_in)
     arrived = travel(back_one)
     copies = call(
         plane_sum_kernel, jax.ShapeDtypeStruct((16, 32, F), jnp.bfloat16), [V], name="plane_sum"
@@ -332,7 +334,7 @@
     whole = lax.all_gather(lax.all_gather(piece[None], "y", tiled=True), MEMBER_AXES, tiled=True)
     shape = lambda *dims: jax.ShapeDtypeStruct(dims, jnp.float32)
     grad_weight_in, grad_bias_in, grad_weight_out, grad_bias_out = call(
-        unpack_kernel, (shape(F, HID), shape(1, HID), shape(HID, F), shape(1, F)), [V], name="unpack"
+        unpack_kernel, (shape(F, HID), shape(HID), shape(HID, F), shape(F)), [V], name="unpack"
     )(whole)
 
     grad_state = call(
@@ -342,9 +344,9 @@
     return (
         grad_state[None],
         grad_weight_in,
-        grad_bias_in[0],
+        grad_bias_in,
         grad_weight_out,
-        grad_bias_out[0],
+        grad_bias_out,
     )
 
 

time: 315 us -> 313 us (level)
  waiting for transfers between devices: 40.3 us -> 44.1 us
    all_to_all x2, waiting for transfers between devices: 27.9 us -> 31.5 us  [travel(): lax.all_to_all(block, SPACE_AXES, split_axis=0, concat_axis=0, tiled=True)]
  transfers between devices with their start and end apart: 3 -> 3, of which waited for: 3 -> 3; matrix products, arithmetic and copies ran while one was open for 3% -> 2% of each run, Pallas kernels for 1% -> 1%
where the time goes in v3:
time: 313 us; the launch traced here: 311 us
  blocking collectives  212 us (68%)
  waiting for transfers between devices  44.1 us (14%)
  starting transfers between devices  28.7 us (9%)
  Pallas kernels  18.2 us (6%)
    all_to_all x4, blocking collectives, travel(): lax.all_to_all(block, SPACE_AXES, split_axis=0, concat_axis=0, tiled=True)  172 us
    all_to_all x2, waiting for transfers between devices, travel(): lax.all_to_all(block, SPACE_AXES, split_axis=0, concat_axis=0, tiled=True)  31.5 us
    all_to_all x2, starting transfers between devices, travel(): lax.all_to_all(block, SPACE_AXES, split_axis=0, concat_axis=0, tiled=True)  25.2 us
    all_to_all x1, blocking collectives, body(): lax.all_to_all(grads_all, PLANE_AXES, split_axis=0, concat_axis=0, tiled=...  14.2 us
    all_gather x1, blocking collectives, body(): lax.all_gather(lax.all_gather(piece[None], 'y', tiled=True), MEMBER_AXES,...  13.1 us
    all_to_all x1, waiting for transfers between devices, body(): lax.all_to_all(copies, 'z', split_axis=0, concat_axis=0, tiled=True)  12.6 us
    all_gather x1, blocking collectives, body(): lax.all_gather(piece[None], 'y', tiled=True)  12.5 us
  transfers between devices with their start and end apart: 3, of which 3 were waited for; matrix products, arithmetic and copies ran while one was open for 2% of the time, Pallas kernels for 1%

profile of v3, /device:TPU:6, one launch (start us, length us, event | category | flops | bytes accessed | tf_op | source)
XLA Modules:
  0.0 311.2 jit_solution(3628317404190462369)
XLA Ops:
  0.6 0.0 copy-start.12
  0.6 2.9 state_synthesis.1
  3.5 18.7 %all-to-all-start = ((bf16[64,32,128]{2,1,0:T(8,128)(2,1)}), bf16[64,32,128]{2,1,0:T(8,128)(2,1)S(1)}, u32[]{:S(2)}, u32[]{:S(2)}) async-start(bf16[64,32,128]{2,1,0:T(8,128)(2,1)} %state_synthesis.1), calls=%async_computation | async-start | bytes 1048576 | tf_op jit(solution)/shard_map/all_to_all | solution.py:236
  22.3 0.1 dynamic_slice.3.waves
  22.4 2.1 fusion.11
  24.5 0.0 copy-start.11
  24.5 0.0 copy-start
  24.6 0.0 copy-start.1
  24.6 0.1 fusion
  24.7 0.0 slice-start
  24.7 0.5 copy.15
  25.3 0.2 convert_element_type.33
  26.1 0.0 copy-done.11
  26.1 1.0 cotangent_synthesis.1.beside
  27.1 0.8 copy-done.4
  28.0 0.2 broadcast_in_dim.11
  28.1 0.0 copy-start.8
  28.2 0.0 copy-start.9
  28.2 0.0 copy-start.10
  28.2 1.7 select_convert_fusion.pick
  29.9 25.2 %all-to-all-done.arrived = bf16[64,32,128]{2,1,0:T(8,128)(2,1)S(1)} async-done(((bf16[64,32,128]{2,1,0:T(8,128)(2,1)}), bf16[64,32,128]{2,1,0:T(8,128)(2,1)S(1)}, u32[]{:S(2)}, u32[]{:S(2)}) %all-to-all-start) | async-done | bytes 524320 | tf_op jit(solution)/shard_map/all_to_all | solution.py:236
  55.1 0.0 copy-done.8
  55.1 0.0 copy-done.10
  55.1 2.3 physics_forward.1
  57.4 37.7 %all_to_all.40.arrived = bf16[64,32,128]{2,1,0:T(8,128)(2,1)S(1)} all-to-all(bf16[64,32,128]{2,1,0:T(8,128)(2,1)S(1)} %get-tuple-element.20), channel_id=1, replica_groups=mesh['x'=4,'core'=2,'z'=16,'y'=4] {'z','y'}, dimensions={0} | all-to-all | bytes 1048576 | tf_op jit(solution)/shard_map/all_to_all | solution.py:236
  95.1 0.0 copy-done.3
  95.1 1.3 state_step.1
  96.4 60.2 %all_to_all.41.arrived = bf16[64,64,128]{2,1,0:T(8,128)(2,1)S(1)} all-to-all(bf16[64,64,128]{2,1,0:T(8,128)(2,1)S(1)} %state_step.1), channel_id=1, replica_groups=mesh['x'=4,'core'=2,'z'=16,'y'=4] {'z','y'}, dimensions={0} | all-to-all | bytes 2097152 | tf_op jit(solution)/shard_map/all_to_all | solution.py:236
  156.6 2.8 physics_turn.1
  159.4 37.1 %all_to_all.42.arrived = bf16[64,32,128]{2,1,0:T(8,128)(2,1)S(1)} all-to-all(bf16[64,32,128]{2,1,0:T(8,128)(2,1)S(1)} %get-tuple-element.22), channel_id=1, replica_groups=mesh['x'=4,'core'=2,'z'=16,'y'=4] {'z','y'}, dimensions={0} | all-to-all | bytes 1048576 | tf_op jit(solution)/shard_map/all_to_all | solution.py:236
  196.4 0.0 copy-done.2
  196.4 1.4 adjoint_step.1
  197.8 0.0 copy-start.6
  197.8 1.0 copy-done.6
  198.8 36.9 %all_to_all.43.arrived = bf16[64,32,128]{2,1,0:T(8,128)(2,1)S(1)} all-to-all(bf16[64,32,128]{2,1,0:T(8,128)(2,1)S(1)} %get-tuple-element.23), channel_id=1, replica_groups=mesh['x'=4,'core'=2,'z'=16,'y'=4] {'z','y'}, dimensions={0} | all-to-all | bytes 1048576 | tf_op jit(solution)/shard_map/all_to_all | solution.py:236
  235.7 1.9 physics_adjoint.1
  237.6 14.2 %all_to_all.44.parts = bf16[32,32,128]{2,1,0:T(8,128)(2,1)S(1)} all-to-all(bf16[32,32,128]{2,1,0:T(8,128)(2,1)S(1)} %get-tuple-element.28), channel_id=1, replica_groups=mesh['x'=4,'core'=2,'z'=16,'y'=4] {'x','core','y'}, dimensions={0} | all-to-all | bytes 524288 | tf_op jit(solution)/shard_map/all_to_all | solution.py:326
  251.8 0.7 plane_sum.1
  252.5 3.5 %all-to-all-start.7 = ((bf16[16,32,128]{2,1,0:T(8,128)(2,1)}), bf16[16,32,128]{2,1,0:T(8,128)(2,1)S(1)}, u32[]{:S(2)}, u32[]{:S(2)}) async-start(bf16[16,32,128]{2,1,0:T(8,128)(2,1)} %plane_sum.1), calls=%async_computation.7 | async-start | bytes 262144 | tf_op jit(solution)/shard_map/all_to_all | solution.py:332
  256.0 1.3 place_adjoint.1
  257.4 12.6 %all-to-all-done.7 = bf16[16,32,128]{2,1,0:T(8,128)(2,1)S(1)} async-done(((bf16[16,32,128]{2,1,0:T(8,128)(2,1)}), bf16[16,32,128]{2,1,0:T(8,128)(2,1)S(1)}, u32[]{:S(2)}, u32[]{:S(2)}) %all-to-all-start.7) | async-done | bytes 131104 | tf_op jit(solution)/shard_map/all_to_all | solution.py:332
  270.0 6.4 %all-to-all-start.5 = ((bf16[64,32,128]{2,1,0:T(8,128)(2,1)}), bf16[64,32,128]{2,1,0:T(8,128)(2,1)S(1)}, u32[]{:S(2)}, u32[]{:S(2)}) async-start(bf16[64,32,128]{2,1,0:T(8,128)(2,1)} %place_adjoint.1), calls=%async_computation.5 | async-start | bytes 1048576 | tf_op jit(solution)/shard_map/all_to_all | solution.py:236
  276.5 12.5 %all-gather = f32[128,128]{1,0:T(8,128)S(1)} all-gather(f32[32,128]{1,0:T(8,128)S(1)} %broadcast_multiply_fusion), channel_id=2, replica_groups=mesh['x'=4,'core'=2,'z'=16,'y'=4] {'y'}, dimensions={0}, use_global_device_ids=true | all-gather | bytes 81920 | tf_op jit(solution)/shard_map/all_gather | solution.py:334
  288.9 13.1 %all_gather.7.whole = f32[32,32,128]{2,1,0:T(8,128)S(1)} all-gather(f32[4,32,128]{2,1,0:T(8,128)S(1)} %bitcast.17), channel_id=1, replica_groups=mesh['x'=4,'core'=2,'z'=16,'y'=4] {'x','core'}, dimensions={0}, use_global_device_ids=true | all-gather | bytes 589824 | tf_op jit(solution)/shard_map/all_gather | solution.py:334
  302.0 0.8 unpack.1
  302.8 6.3 %all-to-all-done.5.arrived = bf16[64,32,128]{2,1,0:T(8,128)(2,1)S(1)} async-done(((bf16[64,32,128]{2,1,0:T(8,128)(2,1)}), bf16[64,32,128]{2,1,0:T(8,128)(2,1)S(1)}, u32[]{:S(2)}, u32[]{:S(2)}) %all-to-all-start.5) | async-done | bytes 524320 | tf_op jit(solution)/shard_map/all_to_all | solution.py:236
  309.1 0.0 copy-done.7
  309.1 1.9 last_analysis.1
  (17 shorter events, 0.1 us)
Async XLA Ops:
  0.6 21.7 %copy-start.12 = (s32[256]{0:T(256)S(1)}, s32[256]{0:T(256)}, u32[]{:S(2)}) copy-start(s32[256]{0:T(256)} %param.13) | copy-start | bytes 3076
  3.5 51.6 %all-to-all-start = ((bf16[64,32,128]{2,1,0:T(8,128)(2,1)}), bf16[64,32,128]{2,1,0:T(8,128)(2,1)S(1)}, u32[]{:S(2)}, u32[]{:S(2)}) async-start(bf16[64,32,128]{2,1,0:T(8,128)(2,1)} %state_synthesis.1), calls=%async_computation | async-start | bytes 1048576 | tf_op jit(solution)/shard_map/all_to_all | solution.py:236
  24.5 1.6 copy-start.11
  24.5 1.6 copy-start
  24.6 1.6 copy-start.1
  24.7 3.3 %slice-start = ((s32[1,2048]{1,0:T(1,128)}), s32[1,512]{1,0:T(1,128)S(1)}, s32[]{:S(2)}) async-start(s32[1,2048]{1,0:T(1,128)} %param.14), calls=%async_computation.8 | async-start | bytes 4096 | tf_op jit(solution)/shard_map/slice | solution.py:251
  27.1 0.8 copy-start.4
  28.1 27.0 %copy-start.8 = (bf16[128,384]{1,0:T(8,128)(2,1)S(1)}, bf16[128,384]{1,0:T(8,128)(2,1)}, u32[]{:S(2)}) copy-start(bf16[128,384]{1,0:T(8,128)(2,1)} %weight_in.5) | copy-start | bytes 294916
  28.2 27.0 %copy-start.9 = (bf16[384,128]{1,0:T(8,128)(2,1)S(1)}, bf16[384,128]{1,0:T(8,128)(2,1)}, u32[]{:S(2)}) copy-start(bf16[384,128]{1,0:T(8,128)(2,1)} %weight_out.5) | copy-start | bytes 294916
  28.2 27.0 %copy-start.10 = (f32[128]{0:T(128)S(1)}, f32[128]{0:T(128)}, u32[]{:S(2)}) copy-start(f32[128]{0:T(128)} %param.19) | copy-start | bytes 1540
  55.1 40.0 %copy-start.3 = (f32[1,4,256,256]{3,2,1,0:T(8,128)S(1)}, f32[1,4,256,256]{3,2,1,0:T(8,128)}, u32[]{:S(2)}) copy-start(f32[1,4,256,256]{3,2,1,0:T(8,128)} %param.10) | copy-start | bytes 3145732
  55.1 40.0 %copy-start.5 = (bf16[64,32,128]{2,1,0:T(8,128)(2,1)S(1)}, bf16[64,32,128]{2,1,0:T(8,128)(2,1)}, u32[]{:S(2)}) copy-start(bf16[64,32,128]{2,1,0:T(8,128)(2,1)} %copy-done.4) | copy-start | bytes 1572868
  156.6 39.8 %copy-start.2 = (f32[1,4,256,256]{3,2,1,0:T(8,128)S(1)}, f32[1,4,256,256]{3,2,1,0:T(8,128)}, u32[]{:S(2)}) copy-start(f32[1,4,256,256]{3,2,1,0:T(8,128)} %param.11) | copy-start | bytes 3145732
  197.8 1.0 copy-start.6
  252.5 17.5 %all-to-all-start.7 = ((bf16[16,32,128]{2,1,0:T(8,128)(2,1)}), bf16[16,32,128]{2,1,0:T(8,128)(2,1)S(1)}, u32[]{:S(2)}, u32[]{:S(2)}) async-start(bf16[16,32,128]{2,1,0:T(8,128)(2,1)} %plane_sum.1), calls=%async_computation.7 | async-start | bytes 262144 | tf_op jit(solution)/shard_map/all_to_all | solution.py:332
  257.4 51.8 %copy-start.7 = (f32[4,256,256]{2,1,0:T(8,128)S(1)}, f32[4,256,256]{2,1,0:T(8,128)}, u32[]{:S(2)}) copy-start(f32[4,256,256]{2,1,0:T(8,128)} %copy-done.6) | copy-start | bytes 3145732
  270.0 39.1 %all-to-all-start.5 = ((bf16[64,32,128]{2,1,0:T(8,128)(2,1)}), bf16[64,32,128]{2,1,0:T(8,128)(2,1)S(1)}, u32[]{:S(2)}, u32[]{:S(2)}) async-start(bf16[64,32,128]{2,1,0:T(8,128)(2,1)} %place_adjoint.1), calls=%async_computation.5 | async-start | bytes 1048576 | tf_op jit(solution)/shard_map/all_to_all | solution.py:236

commit v4 on v3

--- a/solution.py
+++ b/solution.py
@@ -20,6 +20,7 @@
 ACT_TOTAL = 131072
 STEP = 0.5
 SPACE_AXES = ("z", "y")
+TRAVEL_AXES = ("y", "z")
 MEMBER_AXES = ("x", "core")
 PLANE_AXES = ("x", "core", "y")
 VMEM_LIMIT = 12 * 1024 * 1024
@@ -78,13 +79,24 @@
     return copies
 
 
+def send_rows(rows, out):
+    values = rows[...].astype(jnp.bfloat16).reshape(16, 4, ROWS, F)
+    for y in range(4):
+        out[16 * y : 16 * (y + 1), :ROWS, :] = values[:, y]
+
+
+def take_rows(arrived, taken):
+    parts = [arrived[16 * y : 16 * (y + 1)].astype(jnp.float32) for y in range(4)]
+    taken[...] = jnp.stack(parts, axis=1).reshape(taken.shape)
+
+
 def start_kernel(legendre_hbm, state_hbm, out, rows, legendre, state, sems):
     copies = fetch((legendre_hbm, state_hbm), (legendre, state), sems)
     for s in range(SLOTS):
         for one in copies:
             one[s].wait()
         put_slot(rows, s, dot_first(legendre[s], state[s].astype(jnp.bfloat16)))
-    out[...] = rows[...].astype(jnp.bfloat16).reshape(out.shape)
+    send_rows(rows, out)
 
 
 def cotangent_kernel(waves, legendre, state, out, rows):
@@ -92,33 +104,33 @@
         _, truncation = factors(waves[s])
         source = (STEP * (truncation * state[s])).astype(jnp.bfloat16)
         put_slot(rows, s, dot_first(legendre[s], source))
-    out[...] = rows[...].astype(jnp.bfloat16).reshape(out.shape)
+    send_rows(rows, out)
 
 
 def forward_home_kernel(waves, arrived, legendre, state, beside, out, taken, rows):
-    taken[...] = arrived[...].reshape(taken.shape).astype(jnp.float32)
+    take_rows(arrived, taken)
     for s in range(SLOTS):
         damping, truncation = factors(waves[s])
         tendency = dot_last(legendre[s], get_slot(taken, s))
         state_one = truncation * (damping * state[s] + STEP * tendency)
         put_slot(rows, s, dot_first(legendre[s], state_one.astype(jnp.bfloat16)))
-    out[:, :ROWS, :] = rows[...].astype(jnp.bfloat16).reshape(SPACE, ROWS, F)
+    send_rows(rows, out)
     out[:, ROWS:, :] = beside[...]
 
 
 def adjoint_home_kernel(waves, arrived, legendre, cotangent, out, masked_out, taken, rows):
-    taken[...] = arrived[...].reshape(taken.shape).astype(jnp.float32)
+    take_rows(arrived, taken)
     for s in range(SLOTS):
         damping, truncation = factors(waves[s])
         outgoing = damping * (truncation * cotangent[s]) + dot_last(legendre[s], get_slot(taken, s))
         masked = truncation * outgoing
         masked_out[s] = masked
         put_slot(rows, s, dot_first(legendre[s], (STEP * masked).astype(jnp.bfloat16)))
-    out[...] = rows[...].astype(jnp.bfloat16).reshape(out.shape)
+    send_rows(rows, out)
 
 
 def last_home_kernel(waves, arrived, legendre, masked, out_hbm, taken, out, sems):
-    taken[...] = arrived[...].reshape(taken.shape).astype(jnp.float32)
+    take_rows(arrived, taken)
     copies = []
     for s in range(SLOTS):
         damping, _ = factors(waves[s])
@@ -233,7 +245,7 @@
 
 
 def travel(block):
-    return lax.all_to_all(block, SPACE_AXES, split_axis=0, concat_axis=0, tiled=True)
+    return lax.all_to_all(block, TRAVEL_AXES, split_axis=0, concat_axis=0, tiled=True)
 
 
 def fourier_table(wave_ids):
@@ -246,7 +258,8 @@
 
 
 def column_matrix(wave_map, column_list, column_count):
-    table = fourier_table(wave_map).reshape(SPACE, 1, SLOTS * 2, LON)
+    order = wave_map.reshape(16, 4, SLOTS).transpose(1, 0, 2).reshape(-1)
+    table = fourier_table(order).reshape(SPACE, 1, SLOTS * 2, LON)
     table = jnp.broadcast_to(table, (SPACE, LATS, SLOTS * 2, LON)).reshape(SPACE * ROWS, LON)
     columns = column_list[0, :CAPA]
     valid = jnp.arange(CAPA, dtype=jnp.int32) < column_count[0]

time: 313 us -> 313 us (level)
  no operation moved by 1% of the time
where the time goes in v4:
time: 313 us; the launch traced here: 311 us
  blocking collectives  213 us (68%)
  waiting for transfers between devices  42.2 us (13%)
  starting transfers between devices  28.1 us (9%)
  Pallas kernels  18.2 us (6%)
    all_to_all x4, blocking collectives, travel(): lax.all_to_all(block, TRAVEL_AXES, split_axis=0, concat_axis=0, tiled=True)  173 us
    all_to_all x2, waiting for transfers between devices, travel(): lax.all_to_all(block, TRAVEL_AXES, split_axis=0, concat_axis=0, tiled=True)  29.1 us
    all_to_all x2, starting transfers between devices, travel(): lax.all_to_all(block, TRAVEL_AXES, split_axis=0, concat_axis=0, tiled=True)  24.5 us
    all_to_all x1, blocking collectives, body(): lax.all_to_all(grads_all, PLANE_AXES, split_axis=0, concat_axis=0, tiled=...  14.2 us
    all_to_all x1, waiting for transfers between devices, body(): lax.all_to_all(copies, 'z', split_axis=0, concat_axis=0, tiled=True)  13.2 us
    all_gather x1, blocking collectives, body(): lax.all_gather(lax.all_gather(piece[None], 'y', tiled=True), MEMBER_AXES,...  13.1 us
    all_gather x1, blocking collectives, body(): lax.all_gather(piece[None], 'y', tiled=True)  12.5 us
  transfers between devices with their start and end apart: 3, of which 3 were waited for; matrix products, arithmetic and copies ran while one was open for 2% of the time, Pallas kernels for 1%

profile of v4, /device:TPU:6, one launch (start us, length us, event | category | flops | bytes accessed | tf_op | source)
XLA Modules:
  0.0 310.6 jit_solution(15642644673467183353)
XLA Ops:
  0.6 2.9 state_synthesis.1
  3.5 18.7 %all-to-all-start = ((bf16[64,32,128]{2,1,0:T(8,128)(2,1)}), bf16[64,32,128]{2,1,0:T(8,128)(2,1)S(1)}, u32[]{:S(2)}, u32[]{:S(2)}) async-start(bf16[64,32,128]{2,1,0:T(8,128)(2,1)} %state_synthesis.1), calls=%async_computation | async-start | bytes 1048576 | tf_op jit(solution)/shard_map/all_to_all | solution.py:248
  22.3 0.1 reshape.229
  22.4 0.1 dynamic_slice.3.waves
  22.5 0.1 mul.78
  22.6 2.2 fusion.11
  24.8 0.0 copy-start.11
  24.8 0.0 copy-start
  24.8 0.0 copy-start.1
  24.8 0.1 fusion
  24.9 0.0 slice-start
  24.9 0.5 copy.19
  25.5 0.2 convert_element_type.33
  26.3 0.0 copy-done.11
  26.4 1.0 cotangent_synthesis.1.beside
  27.4 0.8 copy-done.4
  28.2 0.0 slice-done
  28.2 0.2 broadcast_in_dim.11
  28.4 0.0 copy-start.8
  28.4 0.0 copy-start.9
  28.4 0.0 copy-start.10
  28.4 1.7 select_convert_fusion.pick
  30.1 23.8 %all-to-all-done.arrived = bf16[64,32,128]{2,1,0:T(8,128)(2,1)S(1)} async-done(((bf16[64,32,128]{2,1,0:T(8,128)(2,1)}), bf16[64,32,128]{2,1,0:T(8,128)(2,1)S(1)}, u32[]{:S(2)}, u32[]{:S(2)}) %all-to-all-start) | async-done | bytes 524320 | tf_op jit(solution)/shard_map/all_to_all | solution.py:248
  54.0 0.0 copy-done.8
  54.0 0.0 copy-done.10
  54.0 2.3 physics_forward.1
  56.3 37.4 %all_to_all.40.arrived = bf16[64,32,128]{2,1,0:T(8,128)(2,1)S(1)} all-to-all(bf16[64,32,128]{2,1,0:T(8,128)(2,1)S(1)} %get-tuple-element.20), channel_id=1, replica_groups=mesh['x'=4,'core'=2,'z'=16,'y'=4] {'y','z'}, dimensions={0} | all-to-all | bytes 1048576 | tf_op jit(solution)/shard_map/all_to_all | solution.py:248
  93.7 0.0 copy-done.5
  93.7 1.3 state_step.1
  95.1 60.2 %all_to_all.41.arrived = bf16[64,64,128]{2,1,0:T(8,128)(2,1)S(1)} all-to-all(bf16[64,64,128]{2,1,0:T(8,128)(2,1)S(1)} %state_step.1), channel_id=1, replica_groups=mesh['x'=4,'core'=2,'z'=16,'y'=4] {'y','z'}, dimensions={0} | all-to-all | bytes 2097152 | tf_op jit(solution)/shard_map/all_to_all | solution.py:248
  155.3 2.8 physics_turn.1
  158.0 38.1 %all_to_all.42.arrived = bf16[64,32,128]{2,1,0:T(8,128)(2,1)S(1)} all-to-all(bf16[64,32,128]{2,1,0:T(8,128)(2,1)S(1)} %get-tuple-element.22), channel_id=1, replica_groups=mesh['x'=4,'core'=2,'z'=16,'y'=4] {'y','z'}, dimensions={0} | all-to-all | bytes 1048576 | tf_op jit(solution)/shard_map/all_to_all | solution.py:248
  196.1 1.4 adjoint_step.1
  197.5 0.0 copy-start.6
  197.5 1.0 copy-done.6
  198.5 37.8 %all_to_all.43.arrived = bf16[64,32,128]{2,1,0:T(8,128)(2,1)S(1)} all-to-all(bf16[64,32,128]{2,1,0:T(8,128)(2,1)S(1)} %get-tuple-element.23), channel_id=1, replica_groups=mesh['x'=4,'core'=2,'z'=16,'y'=4] {'y','z'}, dimensions={0} | all-to-all | bytes 1048576 | tf_op jit(solution)/shard_map/all_to_all | solution.py:248
  236.2 1.9 physics_adjoint.1
  238.1 14.2 %all_to_all.44.parts = bf16[32,32,128]{2,1,0:T(8,128)(2,1)S(1)} all-to-all(bf16[32,32,128]{2,1,0:T(8,128)(2,1)S(1)} %get-tuple-element.28), channel_id=1, replica_groups=mesh['x'=4,'core'=2,'z'=16,'y'=4] {'x','core','y'}, dimensions={0} | all-to-all | bytes 524288 | tf_op jit(solution)/shard_map/all_to_all | solution.py:339
  252.3 0.7 plane_sum.1
  253.0 3.7 %all-to-all-start.7 = ((bf16[16,32,128]{2,1,0:T(8,128)(2,1)}), bf16[16,32,128]{2,1,0:T(8,128)(2,1)S(1)}, u32[]{:S(2)}, u32[]{:S(2)}) async-start(bf16[16,32,128]{2,1,0:T(8,128)(2,1)} %plane_sum.1), calls=%async_computation.7 | async-start | bytes 262144 | tf_op jit(solution)/shard_map/all_to_all | solution.py:345
  256.7 1.3 place_adjoint.1
  258.0 13.2 %all-to-all-done.7 = bf16[16,32,128]{2,1,0:T(8,128)(2,1)S(1)} async-done(((bf16[16,32,128]{2,1,0:T(8,128)(2,1)}), bf16[16,32,128]{2,1,0:T(8,128)(2,1)S(1)}, u32[]{:S(2)}, u32[]{:S(2)}) %all-to-all-start.7) | async-done | bytes 131104 | tf_op jit(solution)/shard_map/all_to_all | solution.py:345
  271.2 5.7 %all-to-all-start.5 = ((bf16[64,32,128]{2,1,0:T(8,128)(2,1)}), bf16[64,32,128]{2,1,0:T(8,128)(2,1)S(1)}, u32[]{:S(2)}, u32[]{:S(2)}) async-start(bf16[64,32,128]{2,1,0:T(8,128)(2,1)} %place_adjoint.1), calls=%async_computation.5 | async-start | bytes 1048576 | tf_op jit(solution)/shard_map/all_to_all | solution.py:248
  277.0 12.5 %all-gather = f32[128,128]{1,0:T(8,128)S(1)} all-gather(f32[32,128]{1,0:T(8,128)S(1)} %broadcast_multiply_fusion), channel_id=2, replica_groups=mesh['x'=4,'core'=2,'z'=16,'y'=4] {'y'}, dimensions={0}, use_global_device_ids=true | all-gather | bytes 81920 | tf_op jit(solution)/shard_map/all_gather | solution.py:347
  289.5 13.1 %all_gather.7.whole = f32[32,32,128]{2,1,0:T(8,128)S(1)} all-gather(f32[4,32,128]{2,1,0:T(8,128)S(1)} %bitcast.18), channel_id=1, replica_groups=mesh['x'=4,'core'=2,'z'=16,'y'=4] {'x','core'}, dimensions={0}, use_global_device_ids=true | all-gather | bytes 589824 | tf_op jit(solution)/shard_map/all_gather | solution.py:347
  302.6 0.8 unpack.1
  303.3 5.2 %all-to-all-done.5.arrived = bf16[64,32,128]{2,1,0:T(8,128)(2,1)S(1)} async-done(((bf16[64,32,128]{2,1,0:T(8,128)(2,1)}), bf16[64,32,128]{2,1,0:T(8,128)(2,1)S(1)}, u32[]{:S(2)}, u32[]{:S(2)}) %all-to-all-start.5) | async-done | bytes 524320 | tf_op jit(solution)/shard_map/all_to_all | solution.py:248
  308.6 1.9 last_analysis.1
  (20 shorter events, 0.1 us)
Async XLA Ops:
  0.6 21.7 %copy-start.12 = (s32[256]{0:T(256)S(1)}, s32[256]{0:T(256)}, u32[]{:S(2)}) copy-start(s32[256]{0:T(256)} %param.13) | copy-start | bytes 3076
  3.5 50.5 %all-to-all-start = ((bf16[64,32,128]{2,1,0:T(8,128)(2,1)}), bf16[64,32,128]{2,1,0:T(8,128)(2,1)S(1)}, u32[]{:S(2)}, u32[]{:S(2)}) async-start(bf16[64,32,128]{2,1,0:T(8,128)(2,1)} %state_synthesis.1), calls=%async_computation | async-start | bytes 1048576 | tf_op jit(solution)/shard_map/all_to_all | solution.py:248
  24.8 1.6 copy-start.11
  24.8 1.6 copy-start
  24.8 1.6 copy-start.1
  24.9 3.3 %slice-start = ((s32[1,2048]{1,0:T(1,128)}), s32[1,512]{1,0:T(1,128)S(1)}, s32[]{:S(2)}) async-start(s32[1,2048]{1,0:T(1,128)} %param.14), calls=%async_computation.8 | async-start | bytes 4096 | tf_op jit(solution)/shard_map/slice | solution.py:264
  27.4 0.8 copy-start.4
  28.4 25.6 %copy-start.8 = (bf16[128,384]{1,0:T(8,128)(2,1)S(1)}, bf16[128,384]{1,0:T(8,128)(2,1)}, u32[]{:S(2)}) copy-start(bf16[128,384]{1,0:T(8,128)(2,1)} %weight_in.5) | copy-start | bytes 294916
  28.4 25.6 %copy-start.9 = (bf16[384,128]{1,0:T(8,128)(2,1)S(1)}, bf16[384,128]{1,0:T(8,128)(2,1)}, u32[]{:S(2)}) copy-start(bf16[384,128]{1,0:T(8,128)(2,1)} %weight_out.5) | copy-start | bytes 294916
  28.4 25.6 %copy-start.10 = (f32[128]{0:T(128)S(1)}, f32[128]{0:T(128)}, u32[]{:S(2)}) copy-start(f32[128]{0:T(128)} %param.19) | copy-start | bytes 1540
  54.0 39.7 %copy-start.3 = (f32[1,4,256,256]{3,2,1,0:T(8,128)S(1)}, f32[1,4,256,256]{3,2,1,0:T(8,128)}, u32[]{:S(2)}) copy-start(f32[1,4,256,256]{3,2,1,0:T(8,128)} %param.10) | copy-start | bytes 3145732
  54.0 39.7 %copy-start.5 = (bf16[64,32,128]{2,1,0:T(8,128)(2,1)S(1)}, bf16[64,32,128]{2,1,0:T(8,128)(2,1)}, u32[]{:S(2)}) copy-start(bf16[64,32,128]{2,1,0:T(8,128)(2,1)} %copy-done.4) | copy-start | bytes 1572868
  155.3 40.8 %copy-start.2 = (f32[1,4,256,256]{3,2,1,0:T(8,128)S(1)}, f32[1,4,256,256]{3,2,1,0:T(8,128)}, u32[]{:S(2)}) copy-start(f32[1,4,256,256]{3,2,1,0:T(8,128)} %param.11) | copy-start | bytes 3145732
  197.5 1.0 copy-start.6
  253.0 18.2 %all-to-all-start.7 = ((bf16[16,32,128]{2,1,0:T(8,128)(2,1)}), bf16[16,32,128]{2,1,0:T(8,128)(2,1)S(1)}, u32[]{:S(2)}, u32[]{:S(2)}) async-start(bf16[16,32,128]{2,1,0:T(8,128)(2,1)} %plane_sum.1), calls=%async_computation.7 | async-start | bytes 262144 | tf_op jit(solution)/shard_map/all_to_all | solution.py:345
  258.0 50.5 %copy-start.7 = (f32[4,256,256]{2,1,0:T(8,128)S(1)}, f32[4,256,256]{2,1,0:T(8,128)}, u32[]{:S(2)}) copy-start(f32[4,256,256]{2,1,0:T(8,128)} %copy-done.6) | copy-start | bytes 3145732
  271.2 37.3 %all-to-all-start.5 = ((bf16[64,32,128]{2,1,0:T(8,128)(2,1)}), bf16[64,32,128]{2,1,0:T(8,128)(2,1)S(1)}, u32[]{:S(2)}, u32[]{:S(2)}) async-start(bf16[64,32,128]{2,1,0:T(8,128)(2,1)} %place_adjoint.1), calls=%async_computation.5 | async-start | bytes 1048576 | tf_op jit(solution)/shard_map/all_to_all | solution.py:248

commit v5 on v3

--- a/solution.py
+++ b/solution.py
@@ -106,15 +106,22 @@
     out[:, ROWS:, :] = beside[...]
 
 
-def adjoint_home_kernel(waves, arrived, legendre, cotangent, out, masked_out, taken, rows):
+def adjoint_home_kernel(
+    waves, arrived, legendre, cotangent, out, masked_hbm, taken, rows, masked, sems
+):
     taken[...] = arrived[...].reshape(taken.shape).astype(jnp.float32)
+    copies = []
     for s in range(SLOTS):
         damping, truncation = factors(waves[s])
         outgoing = damping * (truncation * cotangent[s]) + dot_last(legendre[s], get_slot(taken, s))
-        masked = truncation * outgoing
-        masked_out[s] = masked
-        put_slot(rows, s, dot_first(legendre[s], (STEP * masked).astype(jnp.bfloat16)))
+        masked[s] = truncation * outgoing
+        copies.append(pltpu.make_async_copy(masked.at[s], masked_hbm.at[s], sems.at[s]))
+        copies[s].start()
+    for s in range(SLOTS):
+        put_slot(rows, s, dot_first(legendre[s], (STEP * masked[s]).astype(jnp.bfloat16)))
     out[...] = rows[...].astype(jnp.bfloat16).reshape(out.shape)
+    for copy in copies:
+        copy.wait()
 
 
 def last_home_kernel(waves, arrived, legendre, masked, out_hbm, taken, out, sems):
@@ -280,7 +287,6 @@
     narrow = pltpu.VMEM((CAPA, F), jnp.bfloat16)
     wide = pltpu.VMEM((SPACE, 2 * ROWS, F), jnp.bfloat16)
     full = jax.ShapeDtypeStruct((SLOTS, WAVES, 2 * F), jnp.float32)
-    kept = pltpu.VMEM((SLOTS, WAVES, 2 * F), jnp.float32)
     grads = pltpu.VMEM((32, 32, F), jnp.float32)
     rows = pltpu.VMEM((SPACE * ROWS, F), jnp.float32)
     copied = pltpu.VMEM((SLOTS, WAVES, 2 * F), jnp.float32)
@@ -310,7 +316,12 @@
         travel(both), pick, weight_in, bias_in, weight_out
     )
     adjoint_one, masked_one = call(
-        adjoint_home_kernel, (block, kept), [S, V, V, V], [rows, rows], "adjoint_step"
+        adjoint_home_kernel,
+        (block, pltpu.HBM((SLOTS, WAVES, 2 * F), jnp.float32)),
+        [S, V, V, V],
+        [rows, rows, copied, sems(SLOTS)],
+        "adjoint_step",
+        (V, A),
     )(waves, travel(back_two), legendre, cotangent)
     adjoint_in, grads_all = call(
         last_band_kernel,

time: 313 us -> 313 us (level)
  no operation moved by 1% of the time
where the time goes in v5:
time: 313 us; the launch traced here: 311 us
  blocking collectives  212 us (68%)
  waiting for transfers between devices  44.1 us (14%)
  starting transfers between devices  28.7 us (9%)
  Pallas kernels  18.8 us (6%)
    all_to_all x4, blocking collectives, travel(): lax.all_to_all(block, SPACE_AXES, split_axis=0, concat_axis=0, tiled=True)  172 us
    all_to_all x2, waiting for transfers between devices, travel(): lax.all_to_all(block, SPACE_AXES, split_axis=0, concat_axis=0, tiled=True)  31.5 us
    all_to_all x2, starting transfers between devices, travel(): lax.all_to_all(block, SPACE_AXES, split_axis=0, concat_axis=0, tiled=True)  25.2 us
    all_to_all x1, blocking collectives, body(): lax.all_to_all(grads_all, PLANE_AXES, split_axis=0, concat_axis=0, tiled=...  14.2 us
    all_gather x1, blocking collectives, body(): lax.all_gather(lax.all_gather(piece[None], 'y', tiled=True), MEMBER_AXES,...  13.1 us
    all_to_all x1, waiting for transfers between devices, body(): lax.all_to_all(copies, 'z', split_axis=0, concat_axis=0, tiled=True)  12.6 us
    all_gather x1, blocking collectives, body(): lax.all_gather(piece[None], 'y', tiled=True)  12.5 us
  transfers between devices with their start and end apart: 3, of which 3 were waited for; matrix products, arithmetic and copies ran while one was open for 2% of the time, Pallas kernels for 1%

profile of v5, /device:TPU:6, one launch (start us, length us, event | category | flops | bytes accessed | tf_op | source)
XLA Modules:
  0.0 310.8 jit_solution(4580450348264232602)
XLA Ops:
  0.6 0.0 copy-start.11
  0.6 2.9 state_synthesis.1
  3.5 18.7 %all-to-all-start = ((bf16[64,32,128]{2,1,0:T(8,128)(2,1)}), bf16[64,32,128]{2,1,0:T(8,128)(2,1)S(1)}, u32[]{:S(2)}, u32[]{:S(2)}) async-start(bf16[64,32,128]{2,1,0:T(8,128)(2,1)} %state_synthesis.1), calls=%async_computation | async-start | bytes 1048576 | tf_op jit(solution)/shard_map/all_to_all | solution.py:243
  22.3 0.0 copy-done.11
  22.3 0.1 dynamic_slice.3.waves
  22.4 2.1 fusion.11
  24.5 0.0 copy-start.10
  24.5 0.0 copy-start
  24.6 0.0 copy-start.1
  24.6 0.1 fusion
  24.7 0.0 slice-start
  24.7 0.5 copy.15
  25.3 0.2 convert_element_type.33
  26.1 0.0 copy-done.10
  26.1 0.0 copy-done
  26.1 0.0 copy-done.1
  26.1 1.0 cotangent_synthesis.1.beside
  27.1 0.0 copy-start.4
  27.1 0.8 copy-done.4
  28.0 0.0 slice-done
  28.0 0.2 broadcast_in_dim.11
  28.1 0.0 copy-start.7
  28.2 0.0 copy-start.8
  28.2 0.0 copy-start.9
  28.2 1.7 select_convert_fusion.pick
  29.9 25.2 %all-to-all-done.arrived = bf16[64,32,128]{2,1,0:T(8,128)(2,1)S(1)} async-done(((bf16[64,32,128]{2,1,0:T(8,128)(2,1)}), bf16[64,32,128]{2,1,0:T(8,128)(2,1)S(1)}, u32[]{:S(2)}, u32[]{:S(2)}) %all-to-all-start) | async-done | bytes 524320 | tf_op jit(solution)/shard_map/all_to_all | solution.py:243
  55.1 0.0 copy-done.7
  55.1 0.0 copy-done.8
  55.1 2.3 physics_forward.1
  57.4 37.7 %all_to_all.40.arrived = bf16[64,32,128]{2,1,0:T(8,128)(2,1)S(1)} all-to-all(bf16[64,32,128]{2,1,0:T(8,128)(2,1)S(1)} %get-tuple-element.20), channel_id=1, replica_groups=mesh['x'=4,'core'=2,'z'=16,'y'=4] {'z','y'}, dimensions={0} | all-to-all | bytes 1048576 | tf_op jit(solution)/shard_map/all_to_all | solution.py:243
  95.1 1.3 state_step.1
  96.4 60.2 %all_to_all.41.arrived = bf16[64,64,128]{2,1,0:T(8,128)(2,1)S(1)} all-to-all(bf16[64,64,128]{2,1,0:T(8,128)(2,1)S(1)} %state_step.1), channel_id=1, replica_groups=mesh['x'=4,'core'=2,'z'=16,'y'=4] {'z','y'}, dimensions={0} | all-to-all | bytes 2097152 | tf_op jit(solution)/shard_map/all_to_all | solution.py:243
  156.6 2.8 physics_turn.1
  159.4 37.1 %all_to_all.42.arrived = bf16[64,32,128]{2,1,0:T(8,128)(2,1)S(1)} all-to-all(bf16[64,32,128]{2,1,0:T(8,128)(2,1)S(1)} %get-tuple-element.22), channel_id=1, replica_groups=mesh['x'=4,'core'=2,'z'=16,'y'=4] {'z','y'}, dimensions={0} | all-to-all | bytes 1048576 | tf_op jit(solution)/shard_map/all_to_all | solution.py:243
  196.4 2.0 adjoint_step.1
  198.4 36.9 %all_to_all.43.arrived = bf16[64,32,128]{2,1,0:T(8,128)(2,1)S(1)} all-to-all(bf16[64,32,128]{2,1,0:T(8,128)(2,1)S(1)} %get-tuple-element.23), channel_id=1, replica_groups=mesh['x'=4,'core'=2,'z'=16,'y'=4] {'z','y'}, dimensions={0} | all-to-all | bytes 1048576 | tf_op jit(solution)/shard_map/all_to_all | solution.py:243
  235.3 1.9 physics_adjoint.1
  237.3 14.2 %all_to_all.44.parts = bf16[32,32,128]{2,1,0:T(8,128)(2,1)S(1)} all-to-all(bf16[32,32,128]{2,1,0:T(8,128)(2,1)S(1)} %get-tuple-element.28), channel_id=1, replica_groups=mesh['x'=4,'core'=2,'z'=16,'y'=4] {'x','core','y'}, dimensions={0} | all-to-all | bytes 524288 | tf_op jit(solution)/shard_map/all_to_all | solution.py:337
  251.4 0.7 plane_sum.1
  252.1 3.5 %all-to-all-start.7 = ((bf16[16,32,128]{2,1,0:T(8,128)(2,1)}), bf16[16,32,128]{2,1,0:T(8,128)(2,1)S(1)}, u32[]{:S(2)}, u32[]{:S(2)}) async-start(bf16[16,32,128]{2,1,0:T(8,128)(2,1)} %plane_sum.1), calls=%async_computation.7 | async-start | bytes 262144 | tf_op jit(solution)/shard_map/all_to_all | solution.py:343
  255.7 1.4 place_adjoint.1
  257.0 12.6 %all-to-all-done.7 = bf16[16,32,128]{2,1,0:T(8,128)(2,1)S(1)} async-done(((bf16[16,32,128]{2,1,0:T(8,128)(2,1)}), bf16[16,32,128]{2,1,0:T(8,128)(2,1)S(1)}, u32[]{:S(2)}, u32[]{:S(2)}) %all-to-all-start.7) | async-done | bytes 131104 | tf_op jit(solution)/shard_map/all_to_all | solution.py:343
  269.6 6.4 %all-to-all-start.5 = ((bf16[64,32,128]{2,1,0:T(8,128)(2,1)}), bf16[64,32,128]{2,1,0:T(8,128)(2,1)S(1)}, u32[]{:S(2)}, u32[]{:S(2)}) async-start(bf16[64,32,128]{2,1,0:T(8,128)(2,1)} %place_adjoint.1), calls=%async_computation.5 | async-start | bytes 1048576 | tf_op jit(solution)/shard_map/all_to_all | solution.py:243
  276.1 12.5 %all-gather = f32[128,128]{1,0:T(8,128)S(1)} all-gather(f32[32,128]{1,0:T(8,128)S(1)} %broadcast_multiply_fusion), channel_id=2, replica_groups=mesh['x'=4,'core'=2,'z'=16,'y'=4] {'y'}, dimensions={0}, use_global_device_ids=true | all-gather | bytes 81920 | tf_op jit(solution)/shard_map/all_gather | solution.py:345
  288.6 13.1 %all_gather.7.whole = f32[32,32,128]{2,1,0:T(8,128)S(1)} all-gather(f32[4,32,128]{2,1,0:T(8,128)S(1)} %bitcast.17), channel_id=1, replica_groups=mesh['x'=4,'core'=2,'z'=16,'y'=4] {'x','core'}, dimensions={0}, use_global_device_ids=true | all-gather | bytes 589824 | tf_op jit(solution)/shard_map/all_gather | solution.py:345
  301.7 0.8 unpack.1
  302.4 6.3 %all-to-all-done.5.arrived = bf16[64,32,128]{2,1,0:T(8,128)(2,1)S(1)} async-done(((bf16[64,32,128]{2,1,0:T(8,128)(2,1)}), bf16[64,32,128]{2,1,0:T(8,128)(2,1)S(1)}, u32[]{:S(2)}, u32[]{:S(2)}) %all-to-all-start.5) | async-done | bytes 524320 | tf_op jit(solution)/shard_map/all_to_all | solution.py:243
  308.8 1.9 last_analysis.1
  (15 shorter events, 0.1 us)
Async XLA Ops:
  0.6 21.7 %copy-start.11 = (s32[256]{0:T(256)S(1)}, s32[256]{0:T(256)}, u32[]{:S(2)}) copy-start(s32[256]{0:T(256)} %param.13) | copy-start | bytes 3076
  3.5 51.6 %all-to-all-start = ((bf16[64,32,128]{2,1,0:T(8,128)(2,1)}), bf16[64,32,128]{2,1,0:T(8,128)(2,1)S(1)}, u32[]{:S(2)}, u32[]{:S(2)}) async-start(bf16[64,32,128]{2,1,0:T(8,128)(2,1)} %state_synthesis.1), calls=%async_computation | async-start | bytes 1048576 | tf_op jit(solution)/shard_map/all_to_all | solution.py:243
  24.5 1.6 copy-start.10
  24.5 1.6 copy-start
  24.6 1.6 copy-start.1
  24.7 3.3 %slice-start = ((s32[1,2048]{1,0:T(1,128)}), s32[1,512]{1,0:T(1,128)S(1)}, s32[]{:S(2)}) async-start(s32[1,2048]{1,0:T(1,128)} %param.14), calls=%async_computation.8 | async-start | bytes 4096 | tf_op jit(solution)/shard_map/slice | solution.py:258
  27.1 0.8 copy-start.4
  28.1 27.0 %copy-start.7 = (bf16[128,384]{1,0:T(8,128)(2,1)S(1)}, bf16[128,384]{1,0:T(8,128)(2,1)}, u32[]{:S(2)}) copy-start(bf16[128,384]{1,0:T(8,128)(2,1)} %weight_in.5) | copy-start | bytes 294916
  28.2 27.0 %copy-start.8 = (bf16[384,128]{1,0:T(8,128)(2,1)S(1)}, bf16[384,128]{1,0:T(8,128)(2,1)}, u32[]{:S(2)}) copy-start(bf16[384,128]{1,0:T(8,128)(2,1)} %weight_out.5) | copy-start | bytes 294916
  28.2 26.9 %copy-start.9 = (f32[128]{0:T(128)S(1)}, f32[128]{0:T(128)}, u32[]{:S(2)}) copy-start(f32[128]{0:T(128)} %param.19) | copy-start | bytes 1540
  55.1 40.0 %copy-start.3 = (f32[1,4,256,256]{3,2,1,0:T(8,128)S(1)}, f32[1,4,256,256]{3,2,1,0:T(8,128)}, u32[]{:S(2)}) copy-start(f32[1,4,256,256]{3,2,1,0:T(8,128)} %param.10) | copy-start | bytes 3145732
  55.1 40.0 %copy-start.5 = (bf16[64,32,128]{2,1,0:T(8,128)(2,1)S(1)}, bf16[64,32,128]{2,1,0:T(8,128)(2,1)}, u32[]{:S(2)}) copy-start(bf16[64,32,128]{2,1,0:T(8,128)(2,1)} %copy-done.4) | copy-start | bytes 1572868
  156.6 39.8 %copy-start.2 = (f32[1,4,256,256]{3,2,1,0:T(8,128)S(1)}, f32[1,4,256,256]{3,2,1,0:T(8,128)}, u32[]{:S(2)}) copy-start(f32[1,4,256,256]{3,2,1,0:T(8,128)} %param.11) | copy-start | bytes 3145732
  252.1 17.5 %all-to-all-start.7 = ((bf16[16,32,128]{2,1,0:T(8,128)(2,1)}), bf16[16,32,128]{2,1,0:T(8,128)(2,1)S(1)}, u32[]{:S(2)}, u32[]{:S(2)}) async-start(bf16[16,32,128]{2,1,0:T(8,128)(2,1)} %plane_sum.1), calls=%async_computation.7 | async-start | bytes 262144 | tf_op jit(solution)/shard_map/all_to_all | solution.py:343
  257.0 51.7 %copy-start.6 = (f32[4,256,256]{2,1,0:T(8,128)S(1)}, f32[4,256,256]{2,1,0:T(8,128)}, u32[]{:S(2)}) copy-start(f32[4,256,256]{2,1,0:T(8,128)} %get-tuple-element.27.masked) | copy-start | bytes 3145732
  269.6 39.1 %all-to-all-start.5 = ((bf16[64,32,128]{2,1,0:T(8,128)(2,1)}), bf16[64,32,128]{2,1,0:T(8,128)(2,1)S(1)}, u32[]{:S(2)}, u32[]{:S(2)}) async-start(bf16[64,32,128]{2,1,0:T(8,128)(2,1)} %place_adjoint.1), calls=%async_computation.5 | async-start | bytes 1048576 | tf_op jit(solution)/shard_map/all_to_all | solution.py:243
